TPU v7x, 512 devices: a whole 4x8x8 slice. The times are simulated.
512 devices in a mesh: dp: 16 (over x, z_hi, core), seq: 32 (over z_lo, y).
Axes of the slice: x: 4, y: 8, z: 8 (z_hi: 2, z_lo: 4; z = z_hi * 4 + z_lo), core: 2. Of those that a mesh axis runs over, the one named last changes fastest.
Arguments:
- tokens: bfloat16 [16, 32, 128, 1152], P('dp', 'seq'), may hold values from -6 to 6
- modulation: float32 [16, 6, 1152], P('dp'), may hold values from -0.8 to 0.8
- spatial_project: bfloat16 [1152, 1728], P('seq'), may hold values from -4 to 4
- spatial_merge: bfloat16 [576, 1152], P('seq'), may hold values from -0.25 to 0.25
- temporal_project: bfloat16 [1152, 1728], P('seq'), may hold values from -4 to 4
- temporal_merge: bfloat16 [576, 1152], P('seq'), may hold values from -0.25 to 0.25
- cotangent: bfloat16 [16, 16, 2, 128, 1152], P('dp', None, None, 'seq'), may hold values from -6 to 6
Outputs:
- result: bfloat16 [16, 16, 2, 128, 1152], P('dp', None, None, 'seq')
- token_grads: bfloat16 [16, 32, 128, 1152], P('dp', 'seq')
- merge_grads: float32 [576, 1152], P('seq')
All inputs are finite; a program needn't handle non-finite values.
Results may differ from a plain program's by a relative error of at most 0.035.
Values may be sent and summed in bfloat16 or wider, within the bound.
A program may use at most 64 MiB of HBM per device.

v0:
```python
import jax
import jax.numpy as jnp
from jax import lax
from jax.sharding import PartitionSpec as P

HEAD_DIM = 72


EPSILON = 1e-06
SPATIAL_FORMS = ("qhe,khe->hqk", "hqk,khe->qhe", "hqk,qhe->khe")
TEMPORAL_FORMS = ("fphe,gphe->phfg", "phfg,gphe->fphe", "phfg,fphe->gphe")


def swapped(array, axis, bit):
    return lax.ppermute(array, axis, [(i, i ^ 1 << bit) for i in range(lax.axis_size(axis))])


def modulate(tokens_in, shift_row, scale_row):
    widened = tokens_in.astype(jnp.float32)
    average = jnp.mean(widened, -1, keepdims=True)
    centered = widened - average
    variance = jnp.mean(centered * centered, -1, keepdims=True)
    inverse_std = lax.rsqrt(variance + EPSILON)
    normed = centered * inverse_std
    modulated = (normed * (1.0 + scale_row) + shift_row).astype(jnp.bfloat16)
    return (modulated, normed, inverse_std)


def modulate_back(grad_modulated, normed, inverse_std, scale_row):
    grad_normed = grad_modulated * (1.0 + scale_row)
    first_mean = jnp.mean(grad_normed, -1, keepdims=True)
    second_mean = jnp.mean(grad_normed * normed, -1, keepdims=True)
    return inverse_std * (grad_normed - first_mean - normed * second_mean)


def attend(queries, keys_all, values_all, forms):
    factor = HEAD_DIM ** (-0.5)
    scores = jnp.einsum(forms[0], queries, keys_all, preferred_element_type=jnp.float32) * factor
    probs = jax.nn.softmax(scores, -1)
    weights16 = probs.astype(jnp.bfloat16)
    attended = jnp.einsum(forms[1], weights16, values_all, preferred_element_type=jnp.float32)
    return (attended.astype(jnp.bfloat16), probs)


def attend_back(queries, keys_all, values_all, probs, grad_attended, forms):
    factor = HEAD_DIM ** (-0.5)
    weights16 = probs.astype(jnp.bfloat16)
    grad_probs = jnp.einsum(forms[0], grad_attended, values_all, preferred_element_type=jnp.float32)
    grad_values = jnp.einsum(forms[2], weights16, grad_attended, preferred_element_type=jnp.float32)
    totals = jnp.sum(probs * grad_probs, -1, keepdims=True)
    grad_scores = (probs * (grad_probs - totals) * factor).astype(jnp.bfloat16)
    grad_queries = jnp.einsum(forms[1], grad_scores, keys_all, preferred_element_type=jnp.float32)
    grad_keys = jnp.einsum(forms[2], grad_scores, queries, preferred_element_type=jnp.float32)
    return (grad_queries, grad_keys, grad_values)


def contract_rows(left, right):
    return lax.dot_general(
        left, right, (((1,), (1,)), ((), ())), preferred_element_type=jnp.float32
    )


def body(
    tokens, modulation, spatial_project, spatial_merge, temporal_project, temporal_merge, cotangent
):
    members = lax.axis_size("seq")
    conditioning = modulation[0]
    inner_width = spatial_merge.shape[0] * members
    head_count = inner_width // HEAD_DIM
    space_project, space_merge, time_project, time_merge = (
        lax.all_gather(spatial_project, "seq", axis=0, tiled=True),
        lax.all_gather(spatial_merge, "seq", axis=0, tiled=True),
        lax.all_gather(temporal_project, "seq", axis=0, tiled=True),
        lax.all_gather(temporal_merge, "seq", axis=0, tiled=True),
    )
    local_tokens = tokens[0, 0]
    token_count, model_width = local_tokens.shape
    block_rows = token_count // members
    modulated, normed_space, inverse_space = modulate(
        local_tokens, conditioning[0], conditioning[1]
    )
    packed = jnp.dot(modulated, space_project, preferred_element_type=jnp.float32).astype(
        jnp.bfloat16
    )
    far_pairs = swapped(packed[:, inner_width:], "seq", 0)
    queries = packed[:, :inner_width].reshape(token_count, head_count, HEAD_DIM)
    keys_all = jnp.concatenate(
        [packed[:, inner_width : 2 * inner_width], far_pairs[:, :inner_width]], 0
    )
    keys_all = keys_all.reshape(2 * token_count, head_count, HEAD_DIM)
    values_all = jnp.concatenate([packed[:, 2 * inner_width :], far_pairs[:, inner_width:]], 0)
    values_all = values_all.reshape(2 * token_count, head_count, HEAD_DIM)
    attended, space_probs = attend(queries, keys_all, values_all, SPATIAL_FORMS)
    flat_space = attended.reshape(token_count, inner_width)
    branch = jnp.dot(flat_space, space_merge, preferred_element_type=jnp.float32)
    middle = (local_tokens.astype(jnp.float32) + conditioning[2] * branch).astype(jnp.bfloat16)
    moved = lax.all_to_all(
        middle.reshape(members, block_rows, model_width),
        "seq",
        split_axis=0,
        concat_axis=0,
        tiled=True,
    )
    frame_count = members // 2
    across = moved.reshape(frame_count, 2 * block_rows, model_width)
    patch_count = 2 * block_rows
    modulated_time, normed_time, inverse_time = modulate(across, conditioning[3], conditioning[4])
    packed_time = jnp.dot(
        modulated_time.reshape(token_count, model_width),
        time_project,
        preferred_element_type=jnp.float32,
    ).astype(jnp.bfloat16)
    packed_time = packed_time.reshape(frame_count, patch_count, 3, head_count, HEAD_DIM)
    time_queries, time_keys, time_values = (
        packed_time[:, :, 0],
        packed_time[:, :, 1],
        packed_time[:, :, 2],
    )
    attended_time, time_probs = attend(time_queries, time_keys, time_values, TEMPORAL_FORMS)
    flat_time = attended_time.reshape(token_count, inner_width)
    branch_time = jnp.dot(flat_time, time_merge, preferred_element_type=jnp.float32)
    branch_time = branch_time.reshape(frame_count, patch_count, model_width)
    output = (across.astype(jnp.float32) + conditioning[5] * branch_time).astype(jnp.bfloat16)
    result = output.reshape(1, frame_count, 2, block_rows, model_width)
    grad_result = cotangent[0].reshape(frame_count, patch_count, model_width)
    scaled_time = (conditioning[5] * grad_result.astype(jnp.float32)).astype(jnp.bfloat16)
    scaled_time = scaled_time.reshape(token_count, model_width)
    grad_flat_time = contract_rows(scaled_time, time_merge).astype(jnp.bfloat16)
    grad_part = lax.psum_scatter(
        lax.dot_general(
            flat_time, scaled_time, (((0,), (0,)), ((), ())), preferred_element_type=jnp.float32
        ).astype(jnp.bfloat16),
        "seq",
        scatter_dimension=0,
        tiled=True,
    )
    merge_grads = lax.psum(grad_part, "dp").astype(jnp.float32)
    grad_tq, grad_tk, grad_tv = attend_back(
        time_queries,
        time_keys,
        time_values,
        time_probs,
        grad_flat_time.reshape(frame_count, patch_count, head_count, HEAD_DIM),
        TEMPORAL_FORMS,
    )
    grad_packed_time = jnp.stack([grad_tq, grad_tk, grad_tv], 2).reshape(
        token_count, 3 * inner_width
    )
    grad_modulated_time = contract_rows(grad_packed_time.astype(jnp.bfloat16), time_project)
    grad_modulated_time = grad_modulated_time.reshape(frame_count, patch_count, model_width)
    grad_middle = (
        grad_result.astype(jnp.float32)
        + modulate_back(grad_modulated_time, normed_time, inverse_time, conditioning[4])
    ).astype(jnp.bfloat16)
    returned = lax.all_to_all(
        grad_middle.reshape(members, block_rows, model_width),
        "seq",
        split_axis=0,
        concat_axis=0,
        tiled=True,
    )
    returned = returned.reshape(token_count, model_width)
    scaled_space = (conditioning[2] * returned.astype(jnp.float32)).astype(jnp.bfloat16)
    grad_flat_space = contract_rows(scaled_space, space_merge).astype(jnp.bfloat16)
    grad_sq, grad_keys_all, grad_values_all = attend_back(
        queries,
        keys_all,
        values_all,
        space_probs,
        grad_flat_space.reshape(token_count, head_count, HEAD_DIM),
        SPATIAL_FORMS,
    )
    far_part = jnp.concatenate(
        [
            grad_keys_all[token_count:].reshape(token_count, inner_width),
            grad_values_all[token_count:].reshape(token_count, inner_width),
        ],
        1,
    )
    far_grads = swapped(far_part.astype(jnp.bfloat16), "seq", 0).astype(far_part.dtype)
    grad_keys = (
        grad_keys_all[:token_count].reshape(token_count, inner_width) + far_grads[:, :inner_width]
    )
    grad_values = (
        grad_values_all[:token_count].reshape(token_count, inner_width) + far_grads[:, inner_width:]
    )
    grad_packed = jnp.concatenate(
        [grad_sq.reshape(token_count, inner_width), grad_keys, grad_values], 1
    )
    grad_modulated = contract_rows(grad_packed.astype(jnp.bfloat16), space_project)
    grad_tokens = (
        returned.astype(jnp.float32)
        + modulate_back(grad_modulated, normed_space, inverse_space, conditioning[1])
    ).astype(jnp.bfloat16)
    return (result, grad_tokens.reshape(1, 1, token_count, model_width), merge_grads)


def solution(mesh):
    in_specs = (
        P("dp", "seq", None, None),
        P("dp", None, None),
        P("seq", None),
        P("seq", None),
        P("seq", None),
        P("seq", None),
        P("dp", None, None, "seq", None),
    )
    out_specs = (P("dp", None, None, "seq", None), P("dp", "seq", None, None), P("seq", None))
    return jax.shard_map(body, mesh=mesh, in_specs=in_specs, out_specs=out_specs, check_vma=False)
```

profile of v0, /device:TPU:1, one launch (start us, length us, event | category | flops | bytes accessed | tf_op | source)
XLA Modules:
  0.0 1075.6 jit_solution(18133697046783195577)
XLA Ops:
  7.2 0.7 all-gather.9.cloned.1.call-update
  7.9 0.7 all-gather.11.cloned.1.call-update
  8.7 0.7 all-gather.15.cloned.1.call-update
  9.4 0.5 all-gather.13.cloned.1.call-update
  10.0 0.8 slice_reduce_fusion.1
  10.8 1.1 convert_reduce_fusion
  11.9 1.2 fusion.50
  13.2 145.9 %all-gather.9.cloned.1.call-done = bf16[32,36,1728]{2,1,0:T(8,128)(2,1)} async-done(((bf16[1,36,1728]{2,1,0:T(8,128)(2,1)}), bf16[32,36,1728]{2,1,0:T(8,128)(2,1)}) %all-gather.9.cloned.1.call-update) | async-done | bytes 3981328 | tf_op jit(solution)/shard_map/all_gather | solution.py:71
  159.1 7.3 reshape.209
  166.4 3.9 convolution_convert_fusion.2
  170.3 2.1 collective-permute-start
  172.4 135.3 %all-gather.11.cloned.1.call-done = bf16[32,18,1152]{2,1,0:T(8,128)(2,1)} async-done(((bf16[1,18,1152]{2,1,0:T(8,128)(2,1)}), bf16[32,18,1152]{2,1,0:T(8,128)(2,1)}) %all-gather.11.cloned.1.call-update) | async-done | bytes 1327120 | tf_op jit(solution)/shard_map/all_gather | solution.py:72
  307.7 2.4 reshape.211
  310.3 1.6 fusion.99
  311.9 0.8 convolution_convert_fusion.8
  312.8 0.4 fusion.11
  313.2 0.8 reshape.190
  314.0 6.2 all-to-all-start
  320.3 0.9 reshape.205
  321.1 140.4 %all-gather.15.cloned.1.call-done = bf16[32,18,1152]{2,1,0:T(8,128)(2,1)} async-done(((bf16[1,18,1152]{2,1,0:T(8,128)(2,1)}), bf16[32,18,1152]{2,1,0:T(8,128)(2,1)}) %all-gather.15.cloned.1.call-update) | async-done | bytes 1327120 | tf_op jit(solution)/shard_map/all_gather | solution.py:74
  461.6 3.5 reshape.215
  465.0 1.8 convolution_convert_fusion.10
  467.3 154.1 %all-gather.13.cloned.1.call-done = bf16[32,36,1728]{2,1,0:T(8,128)(2,1)} async-done(((bf16[1,36,1728]{2,1,0:T(8,128)(2,1)}), bf16[32,36,1728]{2,1,0:T(8,128)(2,1)}) %all-gather.13.cloned.1.call-update) | async-done | bytes 3981328 | tf_op jit(solution)/shard_map/all_gather | solution.py:73
  621.4 7.3 reshape.213
  629.5 0.6 copy-done.19
  630.3 3.9 convolution_convert_fusion.1
  634.4 0.9 reshape.191
  635.2 1.0 fusion.96
  636.3 0.7 copy-done.11
  637.0 0.4 fusion.76
  637.4 2.4 fusion.100
  639.7 1.7 fusion.26
  641.4 1.6 fusion.27
  643.1 1.3 fusion.28
  645.0 1.4 convert_element_type.158
  646.4 3.9 fusion.95
  650.6 0.8 reshape.194
  651.4 5.9 all-to-all-start.1
  657.7 0.8 convert_element_type.169
  658.5 1.3 dynamic-slice
  660.4 2.4 reshape.216
  662.8 1.4 fusion.25
  664.2 0.8 copy.36
  665.0 1.9 reshape.202
  666.9 1.9 dot_general.72
  668.8 2.7 convolution_convert_fusion
  671.5 1.8 reshape.207
  673.3 1.6 convolution_convert_fusion.9
  674.9 0.7 copy-done.12
  675.6 1.3 fusion.101
  676.9 2.0 convolution_bitcast_fusion
  678.9 7.8 convolution_bitcast_fusion.1
  686.8 0.8 pad_maximum_fusion.3
  687.6 3.2 collective-permute-start.1
  690.8 1.3 fusion.12
  692.1 0.8 reshape.192
  692.9 7.6 convolution_convert_fusion.7
  700.6 1.0 convert_element_type.165
  701.8 3.8 fusion.94
  705.6 1.0 fusion.58
  706.6 263.2 %all-reduce.3.cloned.1.call-done = bf16[576,1152]{1,0:T(8,128)(2,1)} async-done(((bf16[576,1152]{1,0:T(8,128)(2,1)}), bf16[576,1152]{1,0:T(8,128)(2,1)}) %all-reduce.3.cloned.1.call-update) | async-done | bytes 1327120
  969.9 0.9 constant_dynamic-slice_fusion
  970.8 97.7 %psum.7 = bf16[18,1152]{1,0:T(8,128)(2,1)S(1)} all-reduce(bf16[18,1152]{1,0:T(8,128)(2,1)S(1)} %constant_dynamic-slice_fusion), channel_id=1, replica_groups=mesh['dp'=16,'seq'=32] {'dp'}, use_global_device_ids=true, to_apply=%region_15.0 | all-reduce | flops 20736 | bytes 82944 | tf_op jit(solution)/shard_map/psum | solution.py:137
  1068.4 0.7 convert_element_type.171
  (114 shorter events, 3.5 us)
Async XLA Ops:
  7.2 151.9 %all-gather.9.cloned.1.call-start = ((), (), s32[]{:S(2)}) async-start(), calls=%async_computation.2 | async-start | bytes 4730880 | tf_op jit(solution)/shard_map/all_gather | solution.py:71
  7.9 299.8 %all-gather.11.cloned.1.call-start = ((), (), s32[]{:S(2)}) async-start(), calls=%async_computation.3 | async-start | bytes 1824768 | tf_op jit(solution)/shard_map/all_gather | solution.py:72
  8.6 452.9 %all-gather.15.cloned.1.call-start = ((), (), s32[]{:S(2)}) async-start(), calls=%async_computation.5 | async-start | bytes 1824768 | tf_op jit(solution)/shard_map/all_gather | solution.py:74
  9.4 612.0 %all-gather.13.cloned.1.call-start = ((), (), s32[]{:S(2)}) async-start(), calls=%async_computation.4 | async-start | bytes 4730880 | tf_op jit(solution)/shard_map/all_gather | solution.py:73
  10.8 155.5 %copy-start.27 = (f32[1152]{0:T(1024)}, f32[1152]{0:T(1024)S(1)}, u32[]{:S(2)}) copy-start(f32[1152]{0:T(1024)S(1)} %get-tuple-element.9) | copy-start | bytes 13828
  10.8 301.9 %copy-start.23 = (f32[1152]{0:T(1024)}, f32[1152]{0:T(1024)S(1)}, u32[]{:S(2)}) copy-start(f32[1152]{0:T(1024)S(1)} %get-tuple-element.10) | copy-start | bytes 13828
  10.8 454.2 %copy-start.21 = (f32[1152]{0:T(1024)}, f32[1152]{0:T(1024)S(1)}, u32[]{:S(2)}) copy-start(f32[1152]{0:T(1024)S(1)} %get-tuple-element.7) | copy-start | bytes 13828
  10.8 619.4 %copy-start.25 = (f32[1152]{0:T(1024)}, f32[1152]{0:T(1024)S(1)}, u32[]{:S(2)}) copy-start(f32[1152]{0:T(1024)S(1)} %get-tuple-element.12) | copy-start | bytes 13828
  11.9 154.4 %copy-start.29 = (f32[128]{0:T(128)}, f32[128]{0:T(128)S(1)}, u32[]{:S(2)}) copy-start(f32[128]{0:T(128)S(1)} %broadcast_multiply_fusion.5) | copy-start | bytes 1540
  13.1 153.2 %copy-start.33 = (f32[128]{0:T(128)}, f32[128]{0:T(128)S(1)}, u32[]{:S(2)}) copy-start(f32[128]{0:T(128)S(1)} %add_rsqrt_fusion.1) | copy-start | bytes 1540
  13.2 153.2 %copy-start = (bf16[1,1,128,1152]{3,2,1,0:T(8,128)(2,1)S(1)}, bf16[1,1,128,1152]{3,2,1,0:T(8,128)(2,1)}, u32[]{:S(2)}) copy-start(bf16[1,1,128,1152]{3,2,1,0:T(8,128)(2,1)} %param.7) | copy-start | bytes 884740
  170.3 139.9 %collective-permute-start = (bf16[128,1152]{0,1:T(8,128)(2,1)S(1)}, bf16[128,1152]{0,1:T(8,128)(2,1)S(1)}, u32[]{:S(2)}, u32[]{:S(2)}) collective-permute-start(bf16[128,1152]{0,1:T(8,128)(2,1)S(1)} %slice.97), channel_id=1, source_target_pairs={{0,1},{1,0},{2,3},{3,2},{4,5},{5,4},{6,7},{7,6},{8,9},{9,8},{10,11... | collective-permute-start | bytes 884744 | tf_op jit(solution)/shard_map/ppermute | solution.py:15
  310.2 2.6 copy-start.13
  310.3 1.6 copy-start.5
  310.3 2.4 copy-start.7
  311.9 0.9 copy-start.31
  312.7 7.5 copy-start.2
  314.0 314.7 %all-to-all-start = ((bf16[32,4,1152]{2,1,0:T(4,128)(2,1)}), bf16[32,4,1152]{2,1,0:T(4,128)(2,1)S(1)}, u32[]{:S(2)}, u32[]{:S(2)}) async-start(bf16[32,4,1152]{2,1,0:T(4,128)(2,1)} %reshape.190), calls=%async_computation | async-start | bytes 589824 | tf_op jit(solution)/shard_map/all_to_all | solution.py:97
  628.9 0.6 copy-start.15
  629.5 0.6 copy-start.19
  636.3 0.7 copy-start.11
  636.3 3.5 copy-start.18
  639.7 3.3 copy-start.35
  639.7 1.7 copy-start.17
  643.0 1.4 copy-start.20
  643.0 1.4 copy-start.16
  644.8 1.6 copy-start.26
  646.4 3.9 copy-start.4
  650.3 7.3 copy-start.3
  650.3 7.3 copy-start.22
  651.4 20.1 %all-to-all-start.1 = ((bf16[32,4,1152]{2,1,0:T(4,128)(2,1)}), bf16[32,4,1152]{2,1,0:T(4,128)(2,1)}, u32[]{:S(2)}, u32[]{:S(2)}) async-start(bf16[32,4,1152]{2,1,0:T(4,128)(2,1)} %reshape.194), calls=%async_computation.1 | async-start | bytes 589824 | tf_op jit(solution)/shard_map/all_to_all | solution.py:155
  657.3 312.6 %all-reduce.3.cloned.1.call-start = ((), (), s32[]{:S(2)}) async-start(), calls=%async_computation.6 | async-start | bytes 2654208
  668.8 4.5 copy-start.24
  673.3 2.3 copy-start.8
  674.9 0.7 copy-start.12
  676.9 2.0 copy-start.14
  676.9 2.0 copy-start.32
  678.9 7.9 copy-start.10
  686.7 6.2 copy-start.9
  687.6 5.3 copy-start.6
  687.6 13.0 %collective-permute-start.1 = (bf16[128,1152]{0,1:T(8,128)(2,1)}, bf16[128,1152]{0,1:T(8,128)(2,1)}, u32[]{:S(2)}, u32[]{:S(2)}) collective-permute-start(bf16[128,1152]{0,1:T(8,128)(2,1)} %pad_maximum_fusion.3), channel_id=1, source_target_pairs={{0,1},{1,0},{2,3},{3,2},{4,5},{5,4},{6,7},{7,6},{8,9},{9,8},{10,11... | collective-permute-start | bytes 884744 | tf_op jit(solution)/shard_map/ppermute | solution.py:15
  692.9 8.7 slice-start
  692.9 8.7 slice-start.1
  700.6 1.1 copy-start.28
  700.6 1.1 copy-start.30
  700.6 1.1 copy-start.34
  701.8 3.8 copy-start.1
Sparse Core Ops, SparseCore 0:
  10.1 148.9 all-gather.8
  161.2 146.5 all-gather.10
  309.8 151.7 all-gather.14
  463.5 157.8 all-gather.12
  671.6 298.2 all-reduce.2
where the time goes:
time: 1080 us
  waiting for transfers between devices  842 us (78%)
  blocking collectives  97.7 us (9%)
  matrix products  53.2 us (5%)
  local copies, waits for them, and re-layouts  42.3 us (4%)
  starting transfers between devices  17.8 us (2%)
  between operations  15.2 us (1%)
    unnamed x6, waiting for transfers between devices  266 us
    all_gather x1, waiting for transfers between devices, body(): lax.all_gather(temporal_project, 'seq', axis=0, tiled=True)  154 us
    all_gather x1, waiting for transfers between devices, body(): lax.all_gather(spatial_project, 'seq', axis=0, tiled=True)  146 us
    all_gather x1, waiting for transfers between devices, body(): lax.all_gather(temporal_merge, 'seq', axis=0, tiled=True)  140 us
    all_gather x1, waiting for transfers between devices, body(): lax.all_gather(spatial_merge, 'seq', axis=0, tiled=True)  135 us
    psum x1, blocking collectives, body(): merge_grads = lax.psum(grad_part, 'dp').astype(jnp.float32)  97.7 us
    unnamed x79, local copies, waits for them, and re-layouts  27.3 us
  transfers between devices with their start and end apart: 9, of which 5 were waited for; matrix products, arithmetic and copies ran while one was open for 7% of the time, Pallas kernels for 0%

commit v1 on v0

--- a/solution.py
+++ b/solution.py
@@ -1,9 +1,504 @@
 import jax
 import jax.numpy as jnp
 from jax import lax
+from jax.experimental import pallas as pl
+from jax.experimental.pallas import tpu as pltpu
 from jax.sharding import PartitionSpec as P
 
 HEAD_DIM = 72
+MESH = pl.DeviceIdType.MESH
+LOW, RING = 4, 8
+TILE = (16, 128)
+
+
+class Place:
+    def __init__(self):
+        outer = lax.axis_index("dp")
+        inner = lax.axis_index("seq")
+        self.core = lax.rem(outer, 2)
+        self.high = lax.rem(lax.div(outer, 2), 2)
+        self.x = lax.div(outer, 4)
+        self.low = lax.div(inner, RING)
+        self.y = lax.rem(inner, RING)
+        self.z = self.high * LOW + self.low
+        self.way = 1 - 2 * self.core
+
+    def low_at(self, step):
+        return lax.rem(self.low + step + LOW, LOW)
+
+    def y_at(self, step):
+        return lax.rem(self.y + step + RING, RING)
+
+    def device(self, x=None, y=None, z=None, core=None):
+        x = self.x if x is None else x
+        y = self.y if y is None else y
+        z = self.z if z is None else z
+        core = self.core if core is None else core
+        outer = (x * 2 + lax.div(z, LOW)) * 2 + core
+        return (outer, lax.rem(z, LOW) * RING + y)
+
+    def y_to(self, step):
+        return self.device(y=self.y_at(step))
+
+    def z_to(self, step):
+        return self.device(z=lax.rem(self.z + step + RING, RING))
+
+    def sibling(self):
+        return self.device(core=1 - self.core)
+
+
+def greet(devices):
+    barrier = pltpu.get_barrier_semaphore()
+    for device in devices:
+        pl.semaphore_signal(barrier, inc=1, device_id=device, device_id_type=MESH)
+    pl.semaphore_wait(barrier, len(devices))
+
+
+class Link:
+    def __init__(self, send_sems, recv_sems):
+        self.send_sems, self.recv_sems = send_sems, recv_sems
+        self.count = 0
+        self.started = []
+
+    def number(self):
+        self.count += 1
+        return self.count - 1
+
+    def copy(self, number, source, target, device):
+        return pltpu.make_async_remote_copy(
+            src_ref=source,
+            dst_ref=target,
+            send_sem=self.send_sems.at[number],
+            recv_sem=self.recv_sems.at[number],
+            device_id=device,
+            device_id_type=MESH,
+        )
+
+    def send(self, source, target, device):
+        number = self.number()
+        copy = self.copy(number, source, target, device)
+        copy.start()
+        self.started.append(copy)
+        return number
+
+    def arrived(self, number, target, device):
+        self.copy(number, target, target, device).wait_recv()
+
+    def finish(self):
+        for copy in self.started:
+            copy.wait_send()
+        self.started = []
+
+
+def gather_y_first(place, link, held, first, other, count):
+    way = place.way
+    up, down = place.y_to(1), place.y_to(-1)
+    above, below = place.z_to(1), place.z_to(-1)
+    sibling = place.sibling()
+
+    def one(step):
+        return held.at[place.low, place.y_at(step), pl.ds(first, count)]
+
+    def ring(step, start):
+        return held.at[place.low_at(step), :, pl.ds(start, count)]
+
+    def go(ref, device):
+        return link.send(ref, ref, device)
+
+    plus, minus = go(one(0), up), go(one(0), down)
+    yield
+    for step in (1, 2):
+        link.arrived(plus, one(-step), up)
+        plus = go(one(-step), up)
+        link.arrived(minus, one(step), down)
+        minus = go(one(step), down)
+        yield
+    link.arrived(plus, one(-3), up)
+    link.arrived(minus, one(3), down)
+    last = go(one(-3 * way), place.y_to(way))
+    yield
+    link.arrived(last, one(4), up)
+    plus, minus = go(ring(0, first), above), go(ring(0, first), below)
+    shared = [(go(ring(0, first), sibling), 0)]
+    yield
+    link.arrived(plus, ring(-1, first), above)
+    link.arrived(minus, ring(1, first), below)
+    last = go(ring(-way, first), place.z_to(way))
+    shared.append((go(ring(-1, first), sibling), -1))
+    shared.append((go(ring(1, first), sibling), 1))
+    yield
+    link.arrived(last, ring(2, first), above)
+    shared.append((go(ring(2, first), sibling), 2))
+    yield
+    for number, step in shared:
+        link.arrived(number, ring(step, other), sibling)
+    yield
+
+
+def gather_z_first(place, link, held, first, other, count):
+    way = place.way
+    up, down = place.y_to(1), place.y_to(-1)
+    above, below = place.z_to(1), place.z_to(-1)
+    sibling = place.sibling()
+
+    def one(step):
+        return held.at[place.low_at(step), place.y, pl.ds(first, count)]
+
+    def run(step, start):
+        return held.at[:, place.y_at(step), pl.ds(start, count)]
+
+    def go(ref, device):
+        return link.send(ref, ref, device)
+
+    plus, minus = go(one(0), above), go(one(0), below)
+    yield
+    link.arrived(plus, one(-1), above)
+    link.arrived(minus, one(1), below)
+    last = go(one(-way), place.z_to(way))
+    yield
+    link.arrived(last, one(2), above)
+    plus, minus = go(run(0, first), up), go(run(0, first), down)
+    shared = [(go(run(0, first), sibling), 0)]
+    yield
+    for step in (1, 2):
+        link.arrived(plus, run(-step, first), up)
+        plus = go(run(-step, first), up)
+        link.arrived(minus, run(step, first), down)
+        minus = go(run(step, first), down)
+        shared.append((go(run(-step, first), sibling), -step))
+        shared.append((go(run(step, first), sibling), step))
+        yield
+    link.arrived(plus, run(-3, first), up)
+    link.arrived(minus, run(3, first), down)
+    last = go(run(-3 * way, first), place.y_to(way))
+    shared.append((go(run(-3, first), sibling), -3))
+    shared.append((go(run(3, first), sibling), 3))
+    yield
+    link.arrived(last, run(4, first), up)
+    shared.append((go(run(4, first), sibling), 4))
+    yield
+    for number, step in shared:
+        link.arrived(number, run(step, other), sibling)
+    yield
+
+
+def gather(place, link, held, begin, y_count, z_count):
+    half = y_count + z_count
+    mine, other = begin + place.core * half, begin + (1 - place.core) * half
+    plans = [
+        gather_y_first(place, link, held, mine, other, y_count),
+        gather_z_first(place, link, held, mine + y_count, other + y_count, z_count),
+    ]
+    while plans:
+        for plan in list(plans):
+            if next(plan, plans) is plans:
+                plans.remove(plan)
+        yield
+
+
+def lane_tiles(width):
+    return [(at, min(128, width - at)) for at in range(0, width, 128)]
+
+
+def pack_own(shard, staged, wide, local, begin):
+    rows, width = shard.shape
+    full, rest = rows // 16, rows % 16
+    tiles = lane_tiles(width)
+    number = begin
+    for block in range(full):
+        for at, lanes in tiles:
+            local[number, :, :lanes] = shard[16 * block : 16 * block + 16, at : at + lanes]
+            number += 1
+    per = 16 // rest
+    wide[:rest, :width] = shard[16 * full :, :].astype(jnp.float32)
+    groups = -(-len(tiles) // per)
+    for index, (at, lanes) in enumerate(tiles):
+        staged[index // per, pl.ds(rest * (index % per), rest), :lanes] = wide[
+            :rest, at : at + lanes
+        ]
+    for group in range(groups):
+        local[number + group] = staged[group].astype(jnp.bfloat16)
+
+
+def hold_own(place, local, held, begin, count):
+    mine = pl.ds(begin + place.core * (count // 2), count // 2)
+    held[place.low, place.y, mine] = local[mine]
+
+
+def unpack_all(held, begin, rows, width, stage, out):
+    full, rest = rows // 16, rows % 16
+    tiles = lane_tiles(width)
+    per = 16 // rest
+    several = 4 if rows == 36 else 8
+    block = several * rows
+
+    def step(index, carry):
+        low, y = lax.div(index * several, RING), lax.rem(index * several, RING)
+        for shard in range(several):
+            top = shard * rows
+            for part in range(full):
+                for tile, (at, lanes) in enumerate(tiles):
+                    value = held[low, y + shard, begin + part * len(tiles) + tile]
+                    stage[top + 16 * part : top + 16 * part + 16, at : at + lanes] = value.astype(
+                        jnp.float32
+                    )[:, :lanes]
+            for group in range(-(-len(tiles) // per)):
+                value = held[low, y + shard, begin + full * len(tiles) + group]
+                value = value.astype(jnp.float32)
+                for piece in range(per):
+                    tile = group * per + piece
+                    if tile < len(tiles):
+                        at, lanes = tiles[tile]
+                        stage[top + 16 * full : top + rows, at : at + lanes] = value[
+                            rest * piece : rest * piece + rest, :lanes
+                        ]
+        out[pl.ds(pl.multiple_of(index * block, 16), block), :] = stage[:block, :width].astype(
+            jnp.bfloat16
+        )
+        return carry
+
+    lax.fori_loop(0, 32 // several, step, 0)
+
+
+PROJECT_TILES, MERGE_TILES = 32, 12
+HELD_TILES = 2 * (PROJECT_TILES + MERGE_TILES)
+GATHER_COPIES = 32
+
+
+def gather_kernel(
+    space_project,
+    space_merge,
+    time_project,
+    time_merge,
+    space_project_all,
+    space_merge_all,
+    time_project_all,
+    time_merge_all,
+    held,
+    staged,
+    wide,
+    stage,
+    local,
+    send_sems,
+    recv_sems,
+):
+    place = Place()
+    greet(
+        [place.y_to(1), place.y_to(-1), place.z_to(1), place.z_to(-1), place.sibling()]
+    )
+    starts = (0, PROJECT_TILES, PROJECT_TILES + MERGE_TILES, 2 * PROJECT_TILES + MERGE_TILES)
+    shards = (space_project, space_merge, time_project, time_merge)
+    links = [Link(send_sems.at[i], recv_sems.at[i]) for i in range(3)]
+    pack_own(space_project, staged, wide, local, starts[0])
+    hold_own(place, local, held, starts[0], 32)
+    plans = [gather(place, links[0], held, 0, 9, 7)]
+    next(plans[0])
+    for shard, start in zip(shards[1:], starts[1:]):
+        pack_own(shard, staged, wide, local, start)
+    hold_own(place, local, held, starts[1], 12)
+    hold_own(place, local, held, starts[2], 44)
+    plans.append(gather(place, links[1], held, starts[1], 4, 2))
+    plans.append(gather(place, links[2], held, starts[2], 13, 9))
+    live = list(plans)
+    while live:
+        for plan in list(live):
+            if next(plan, live) is live:
+                live.remove(plan)
+    unpack_all(held, starts[0], 36, 1728, stage, space_project_all)
+    unpack_all(held, starts[1], 18, 1152, stage, space_merge_all)
+    unpack_all(held, starts[2], 36, 1728, stage, time_project_all)
+    unpack_all(held, starts[3], 18, 1152, stage, time_merge_all)
+    for link in links:
+        link.finish()
+
+
+def gather_weights(space_project, space_merge, time_project, time_merge):
+    vmem = pl.BlockSpec(memory_space=pltpu.VMEM)
+    project = jax.ShapeDtypeStruct((1152, 1728), jnp.bfloat16)
+    merge = jax.ShapeDtypeStruct((576, 1152), jnp.bfloat16)
+    return pl.pallas_call(
+        gather_kernel,
+        out_shape=[project, merge, project, merge],
+        in_specs=[vmem] * 4,
+        out_specs=[vmem] * 4,
+        scratch_shapes=[
+            pltpu.VMEM((LOW, RING, HELD_TILES) + TILE, jnp.bfloat16),
+            pltpu.VMEM((4,) + TILE, jnp.float32),
+            pltpu.VMEM((8, 1792), jnp.float32),
+            pltpu.VMEM((144, 1792), jnp.float32),
+            pltpu.VMEM((HELD_TILES,) + TILE, jnp.bfloat16),
+            pltpu.SemaphoreType.DMA((3, GATHER_COPIES)),
+            pltpu.SemaphoreType.DMA((3, GATHER_COPIES)),
+        ],
+        compiler_params=pltpu.CompilerParams(
+            collective_id=0, has_side_effects=True, vmem_limit_bytes=56 * 1024 * 1024
+        ),
+        cost_estimate=pl.CostEstimate(flops=0, bytes_accessed=22_000_000, transcendentals=0),
+        name="gather_weights",
+    )(space_project, space_merge, time_project, time_merge)
+
+
+REDUCE_COPIES = 16
+
+
+def reduce_plan(place, link, packed, near, total, long_out, long_in, short_out, short_in, small, final):
+    way, half = place.way, MERGE_TILES // 2
+    mine, other = place.core * half, (1 - place.core) * half
+    sibling = place.sibling()
+    number = link.send(packed.at[:, :, pl.ds(other, half)], near, sibling)
+    yield
+    link.arrived(number, near, sibling)
+
+    def add(low, carry):
+        for y in range(RING):
+            total[low, y] = packed[low, y, pl.ds(mine, half)].astype(jnp.float32) + near[
+                low, y
+            ].astype(jnp.float32)
+        return carry
+
+    lax.fori_loop(0, LOW, add, 0)
+    there, back = place.y_to(way), place.y_to(-way)
+    for step in range(4):
+        value = total[:, place.y_at((4 - step) * way)]
+        if step:
+            link.arrived(long_number, long_in.at[step - 1], there)
+            value = value + long_in[step - 1].astype(jnp.float32)
+        long_out[step] = value.astype(jnp.bfloat16)
+        long_number = link.send(long_out.at[step], long_in.at[step], there)
+        if step < 3:
+            value = total[:, place.y_at((step - 3) * way)]
+            if step:
+                link.arrived(short_number, short_in.at[step - 1], back)
+                value = value + short_in[step - 1].astype(jnp.float32)
+            short_out[step] = value.astype(jnp.bfloat16)
+            short_number = link.send(short_out.at[step], short_in.at[step], back)
+        yield
+    link.arrived(short_number, short_in.at[2], back)
+    link.arrived(long_number, long_in.at[3], there)
+    small[pl.ds(0, 4)] = (
+        total[:, place.y] + long_in[3].astype(jnp.float32) + short_in[2].astype(jnp.float32)
+    )
+    parity, upper = lax.rem(place.low, 2), lax.div(place.low, 2)
+    device = place.device(z=place.z + 1 - 2 * parity)
+    numbers = [
+        link.send(small.at[1 - parity + 2 * k], small.at[4 + k], device) for k in range(2)
+    ]
+    yield
+    for k in range(2):
+        link.arrived(numbers[k], small.at[4 + k], device)
+        small[6 + k] = small[parity + 2 * k] + small[4 + k]
+    device = place.device(z=place.z + 2 - 4 * upper)
+    number = link.send(small.at[7 - upper], small.at[8], device)
+    yield
+    link.arrived(number, small.at[8], device)
+    small[9] = small[6 + upper] + small[8]
+    at = 9
+    for device in (
+        place.device(z=lax.rem(place.z + LOW, RING)),
+        place.device(x=place.x + 1 - 2 * lax.rem(place.x, 2)),
+        place.device(x=lax.rem(place.x + 2, 4)),
+    ):
+        number = link.send(small.at[at], small.at[at + 1], device)
+        yield
+        link.arrived(number, small.at[at + 1], device)
+        small[at + 2] = small[at] + small[at + 1]
+        at += 2
+    final[pl.ds(mine, half)] = small[at]
+    number = link.send(final.at[pl.ds(mine, half)], final.at[pl.ds(mine, half)], sibling)
+    yield
+    link.arrived(number, final.at[pl.ds(other, half)], sibling)
+
+
+def reduce_partners(place):
+    parity, upper = lax.rem(place.low, 2), lax.div(place.low, 2)
+    return [
+        place.sibling(),
+        place.y_to(1),
+        place.y_to(-1),
+        place.device(z=place.z + 1 - 2 * parity),
+        place.device(z=place.z + 2 - 4 * upper),
+        place.device(z=lax.rem(place.z + LOW, RING)),
+        place.device(x=place.x + 1 - 2 * lax.rem(place.x, 2)),
+        place.device(x=lax.rem(place.x + 2, 4)),
+    ]
+
+
+def pack_partial(part, stage, staged, packed):
+    def step(low, carry):
+        stage[...] = part[pl.ds(pl.multiple_of(low * 144, 16), 144), :].astype(jnp.float32)
+        staged[...] = jnp.zeros_like(staged)
+        for y in range(RING):
+            for tile in range(9):
+                at = 128 * tile
+                packed[low, y, tile] = stage[18 * y : 18 * y + 16, at : at + 128].astype(
+                    jnp.bfloat16
+                )
+                staged[y, tile // 8, 2 * (tile % 8) : 2 * (tile % 8) + 2, :] = stage[
+                    18 * y + 16 : 18 * y + 18, at : at + 128
+                ]
+            for group in range(3):
+                packed[low, y, 9 + group] = staged[y, group].astype(jnp.bfloat16)
+        return carry
+
+    lax.fori_loop(0, LOW, step, 0)
+
+
+def unpack_final(final, out):
+    for tile in range(9):
+        at = 128 * tile
+        out[0:16, at : at + 128] = final[tile]
+        out[16:18, at : at + 128] = final[9 + tile // 8, 2 * (tile % 8) : 2 * (tile % 8) + 2, :]
+
+
+def reduce_kernel(
+    part, out, stage, staged, packed, near, total, long_out, long_in, short_out, short_in, small,
+    final, send_sems, recv_sems,
+):
+    place = Place()
+    greet(reduce_partners(place))
+    link = Link(send_sems, recv_sems)
+    pack_partial(part, stage, staged, packed)
+    for _ in reduce_plan(
+        place, link, packed, near, total, long_out, long_in, short_out, short_in, small, final
+    ):
+        pass
+    unpack_final(final, out)
+    link.finish()
+
+
+def reduce_scratch():
+    half = MERGE_TILES // 2
+    return [
+        pltpu.VMEM((144, 1152), jnp.float32),
+        pltpu.VMEM((RING, 3) + TILE, jnp.float32),
+        pltpu.VMEM((LOW, RING, MERGE_TILES) + TILE, jnp.bfloat16),
+        pltpu.VMEM((LOW, RING, half) + TILE, jnp.bfloat16),
+        pltpu.VMEM((LOW, RING, half) + TILE, jnp.float32),
+        pltpu.VMEM((4, LOW, half) + TILE, jnp.bfloat16),
+        pltpu.VMEM((4, LOW, half) + TILE, jnp.bfloat16),
+        pltpu.VMEM((3, LOW, half) + TILE, jnp.bfloat16),
+        pltpu.VMEM((3, LOW, half) + TILE, jnp.bfloat16),
+        pltpu.VMEM((16, half) + TILE, jnp.float32),
+        pltpu.VMEM((MERGE_TILES,) + TILE, jnp.float32),
+        pltpu.SemaphoreType.DMA((REDUCE_COPIES,)),
+        pltpu.SemaphoreType.DMA((REDUCE_COPIES,)),
+    ]
+
+
+def reduce_grads(part):
+    vmem = pl.BlockSpec(memory_space=pltpu.VMEM)
+    return pl.pallas_call(
+        reduce_kernel,
+        out_shape=jax.ShapeDtypeStruct((18, 1152), jnp.float32),
+        in_specs=[vmem],
+        out_specs=vmem,
+        scratch_shapes=reduce_scratch(),
+        compiler_params=pltpu.CompilerParams(
+            collective_id=1, has_side_effects=True, vmem_limit_bytes=56 * 1024 * 1024
+        ),
+        cost_estimate=pl.CostEstimate(flops=0, bytes_accessed=8_000_000, transcendentals=0),
+        name="reduce_grads",
+    )(part)
 
 
 EPSILON = 1e-06
@@ -67,11 +562,8 @@
     conditioning = modulation[0]
     inner_width = spatial_merge.shape[0] * members
     head_count = inner_width // HEAD_DIM
-    space_project, space_merge, time_project, time_merge = (
-        lax.all_gather(spatial_project, "seq", axis=0, tiled=True),
-        lax.all_gather(spatial_merge, "seq", axis=0, tiled=True),
-        lax.all_gather(temporal_project, "seq", axis=0, tiled=True),
-        lax.all_gather(temporal_merge, "seq", axis=0, tiled=True),
+    space_project, space_merge, time_project, time_merge = gather_weights(
+        spatial_project, spatial_merge, temporal_project, temporal_merge
     )
     local_tokens = tokens[0, 0]
     token_count, model_width = local_tokens.shape
@@ -126,15 +618,11 @@
     scaled_time = (conditioning[5] * grad_result.astype(jnp.float32)).astype(jnp.bfloat16)
     scaled_time = scaled_time.reshape(token_count, model_width)
     grad_flat_time = contract_rows(scaled_time, time_merge).astype(jnp.bfloat16)
-    grad_part = lax.psum_scatter(
+    merge_grads = reduce_grads(
         lax.dot_general(
             flat_time, scaled_time, (((0,), (0,)), ((), ())), preferred_element_type=jnp.float32
-        ).astype(jnp.bfloat16),
-        "seq",
-        scatter_dimension=0,
-        tiled=True,
-    )
-    merge_grads = lax.psum(grad_part, "dp").astype(jnp.float32)
+        ).astype(jnp.bfloat16)
+    )
     grad_tq, grad_tk, grad_tv = attend_back(
         time_queries,
         time_keys,

time: 1080 us -> 232 us (0.21)
  waiting for transfers between devices: 842 us -> 22.7 us
  Pallas kernels: 0 us -> 118 us
  blocking collectives: 97.7 us -> 0 us
  local copies, waits for them, and re-layouts: 42.3 us -> 11.4 us
  between operations: 15.2 us -> 1.33 us
    all_gather x4 -> x0, waiting for transfers between devices: 576 us -> none  [the longest x1 154 us: body(): lax.all_gather(temporal_project, 'seq', axis=0, tiled=True)]
    unnamed x6 -> x0, waiting for transfers between devices: 266 us -> none
    pallas_call x0 -> x2, Pallas kernels: none -> 118 us  [the longest x1 72.3 us: gather_weights(): pl.pallas_call(gather_kernel, out_shape=[project, merge, project, merge],...]
    psum x1 -> x0, blocking collectives: 97.7 us -> none  [body(): merge_grads = lax.psum(grad_part, 'dp').astype(jnp.float32)]
    unnamed x79 -> x71, local copies, waits for them, and re-layouts: 27.3 us -> 2.04 us
  transfers between devices with their start and end apart: 9 -> 4, of which waited for: 5 -> 3; matrix products, arithmetic and copies ran while one was open for 7% -> 7% of each run, Pallas kernels for 0% -> 20%
where the time goes in v1:
time: 232 us; the launch traced here: 231 us
  Pallas kernels  118 us (51%)
  matrix products  51.2 us (22%)
  waiting for transfers between devices  22.7 us (10%)
  starting transfers between devices  18.9 us (8%)
  local copies, waits for them, and re-layouts  11.4 us (5%)
  other arithmetic  7.26 us (3%)
    pallas_call x1, Pallas kernels, gather_weights(): pl.pallas_call(gather_kernel, out_shape=[project, merge, project, merge],...  72.3 us
    pallas_call x1, Pallas kernels, reduce_grads(): pl.pallas_call(reduce_kernel, out_shape=jax.ShapeDtypeStruct((18, 1152),...  45.7 us
    dot_general x2, matrix products, attend_back(): jnp.einsum(forms[1], grad_scores, keys_all, preferred_element_type=jnp.fl...  10.1 us
    dot_general x2, matrix products, attend_back(): jnp.einsum(forms[2], grad_scores, queries, preferred_element_type=jnp.flo...  10.1 us
    dot_general x4, matrix products, contract_rows(): lax.dot_general(left, right, (((1,), (1,)), ((), ())), preferred_element_...  9.88 us
    all_to_all x1, waiting for transfers between devices, body(): lax.all_to_all(middle.reshape(members, block_rows, model_width), 'seq', s...  8.77 us
    all_to_all x1, waiting for transfers between devices, body(): lax.all_to_all(grad_middle.reshape(members, block_rows, model_width), 'se...  7.92 us
    ppermute x2, starting transfers between devices, swapped(): lax.ppermute(array, axis, [(i, i ^ 1 << bit) for i in range(lax.axis_size...  7.75 us
  transfers between devices with their start and end apart: 4, of which 3 were waited for; matrix products, arithmetic and copies ran while one was open for 7% of the time, Pallas kernels for 20%

profile of v1, /device:TPU:1, one launch (start us, length us, event | category | flops | bytes accessed | tf_op | source)
XLA Modules:
  0.0 230.8 jit_solution(6590600817657659722)
XLA Ops:
  0.6 0.8 slice_reduce_fusion.1
  1.5 1.1 convert_reduce_fusion
  2.6 1.2 fusion.51
  3.8 72.3 %gather_weights.1 = (bf16[1152,1728]{1,0:T(8,128)(2,1)}, bf16[576,1152]{1,0:T(8,128)(2,1)}, bf16[1152,1728]{1,0:T(8,128)(2,1)}, bf16[576,1152]{1,0:T(8,128)(2,1)}) custom-call(bf16[36,1728]{1,0:T(8,128)(2,1)} %space_project.1, bf16[18,1152]{1,0:T(8,128)(2,1)} %space_merge.1, bf16[36,1728]{1,0:T(8,128)(2,1)} %time_project.1, bf16[18,1152]{1,0:T(8,128)(2,1)} %time_merge.1), custom_call_target="tpu_custom_call" | custom-call | bytes 22000000 | tf_op jit(solution)/shard_map/gather_weights/pallas_call | solution.py:319
  76.1 4.0 %convolution_convert_fusion.2 = bf16[128,1728]{0,1:T(8,128)(2,1)S(1)} fusion(bf16[1152,1728]{1,0:T(8,128)(2,1)} %get-tuple-element.7, bf16[1,1,128,1152]{3,2,1,0:T(8,128)(2,1)} %param.7, f32[1152]{0:T(1024)S(1)} %get-tuple-element.16, f32[1152]{0:T(1024)S(1)} %get-tuple-element.17, f32[128]{0:T(128)S(1)} %add_rsqrt_fusion.1, ...), kind=kOutput, calls=%fused_computation.16 | convolution fusion | flops 510713856 | bytes 4728832 | tf_op jit(solution)/shard_map/dot_general | solution.py:574
  80.1 3.6 %collective-permute-start = (bf16[128,1152]{0,1:T(8,128)(2,1)S(1)}, bf16[128,1152]{0,1:T(8,128)(2,1)S(1)}, u32[]{:S(2)}, u32[]{:S(2)}) collective-permute-start(bf16[128,1152]{0,1:T(8,128)(2,1)S(1)} %slice.97), channel_id=1, source_target_pairs={{0,1},{1,0},{2,3},{3,2},{4,5},{5,4},{6,7},{7,6},{8,9},{9,8},{10,11... | collective-permute-start | bytes 884744 | tf_op jit(solution)/shard_map/ppermute | solution.py:510
  83.8 6.0 %collective-permute-done = bf16[128,1152]{0,1:T(8,128)(2,1)S(1)} collective-permute-done((bf16[128,1152]{0,1:T(8,128)(2,1)S(1)}, bf16[128,1152]{0,1:T(8,128)(2,1)S(1)}, u32[]{:S(2)}, u32[]{:S(2)}) %collective-permute-start) | collective-permute-done | bytes 294944 | tf_op jit(solution)/shard_map/ppermute | solution.py:510
  89.8 0.1 pad_maximum_fusion.1
  89.9 1.6 fusion.100
  91.5 0.8 convolution_convert_fusion.8
  92.4 0.1 copy-done
  92.5 0.5 copy-done.2
  92.9 0.4 fusion.11
  93.4 0.8 reshape.190
  94.2 5.0 %all-to-all-start = ((bf16[32,4,1152]{2,1,0:T(4,128)(2,1)}), bf16[32,4,1152]{2,1,0:T(4,128)(2,1)S(1)}, u32[]{:S(2)}, u32[]{:S(2)}) async-start(bf16[32,4,1152]{2,1,0:T(4,128)(2,1)} %reshape.190), calls=%async_computation | async-start | bytes 589824 | tf_op jit(solution)/shard_map/all_to_all | solution.py:589
  99.2 0.9 reshape.205
  100.1 0.5 convolution_convert_fusion.10
  100.6 0.2 copy.24
  100.8 1.0 reshape.193
  101.8 8.8 %all-to-all-done = bf16[32,4,1152]{2,1,0:T(4,128)(2,1)S(1)} async-done(((bf16[32,4,1152]{2,1,0:T(4,128)(2,1)}), bf16[32,4,1152]{2,1,0:T(4,128)(2,1)S(1)}, u32[]{:S(2)}, u32[]{:S(2)}) %all-to-all-start) | async-done | bytes 294944 | tf_op jit(solution)/shard_map/all_to_all | solution.py:589
  110.5 0.2 convert_reduce_fusion.1
  110.7 0.1 div.49
  110.8 0.3 multiply_reduce_fusion.3
  111.2 0.1 rsqrt.25
  111.4 4.6 %convolution_convert_fusion.1 = bf16[128,1728]{0,1:T(8,128)(2,1)} fusion(bf16[1152,1728]{1,0:T(8,128)(2,1)} %get-tuple-element.9, f32[128,1152]{1,0:T(8,128)S(1)} %reshape.204, f32[1152]{0:T(1024)S(1)} %get-tuple-element.19, f32[1152]{0:T(1024)S(1)} %get-tuple-element.20, f32[128]{0:T(128)S(1)} %rsqrt.25, f32[128]{0:T(128)S(1)} %div.49), kind=kOutput, calls=%fused_computation.15 | convolution fusion | flops 510566400 | bytes 5023744 | tf_op jit(solution)/shard_map/dot_general | solution.py:600
  116.0 1.2 copy.18
  117.2 0.9 reshape.191
  118.1 1.0 fusion.97
  119.1 0.7 copy-done.13
  119.8 0.4 fusion.77
  120.2 2.4 %fusion.101 = (f32[8,8,16]{2,1,0:T(8,128)S(1)}, f32[8,8,16,16]{2,3,1,0:T(8,128)}) fusion(bf16[16,8,1,8,72]{4,3,2,1,0:T(8,128)(2,1)} %get-tuple-element.22, bf16[16,8,1,8,72]{4,3,2,1,0:T(8,128)(2,1)} %get-tuple-element.21), kind=kOutput, calls=%fused_computation.152 | convolution fusion | flops 2408463 | bytes 364544 | tf_op jit(solution)/shard_map/sub | solution.py:534
  122.6 2.5 %fusion.27 = bf16[16,8,1,8,72]{4,0,3,1,2:T(8,128)(2,1)} fusion(f32[8,8,16,16]{2,3,1,0:T(8,128)S(1)} %fusion.77, bf16[16,8,1,8,72]{4,3,2,1,0:T(8,128)(2,1)} %get-tuple-element.21, f32[8,8,16,16]{2,3,1,0:T(8,128)} %get-tuple-element.34, f32[8,8,16]{2,1,0:T(8,128)S(1)} %get-tuple-element.33), kind=kOutput, calls=%fused_computation.39 | convolution fusion | flops 2548751 | bytes 430080 | tf_op jit(solution)/shard_map/phfg,gphe->fphe/dot_general | solution.py:547
  125.1 2.3 fusion.28
  127.4 1.4 fusion.29
  128.8 0.1 rsqrt.26
  128.8 0.1 div.54
  128.9 0.2 pad_maximum_fusion
  129.1 0.2 copy.28
  129.3 0.5 convert_element_type.155
  129.9 3.7 %fusion.96 = (f32[16,8]{1,0:T(8,128)S(1)}, f32[16,8]{1,0:T(8,128)S(1)}, f32[16,8,1152]{2,1,0:T(8,128)S(1)}) fusion(f32[16,8]{1,0:T(8,128)S(1)} %rsqrt.26, f32[16,8,1152]{2,1,0:T(8,128)S(1)} %reshape.203, f32[16,8]{1,0:T(8,128)S(1)} %div.54, f32[1152]{0:T(1024)S(1)} %get-tuple-element.20, bf16[16,8,1728]{2,1,0:T(8,128)(2,1)S(1)} %convert_element_type.155, ...), kind=kOutput, calls=%fused_computation.147 | convolution fusion | flops 510492416 | bytes 5609984 | tf_op jit(solution)/shard_map/dot_general | solution.py:553
  133.7 0.3 add_convert_fusion
  134.0 0.8 reshape.194
  134.8 6.1 %all-to-all-start.1 = ((bf16[32,4,1152]{2,1,0:T(4,128)(2,1)}), bf16[32,4,1152]{2,1,0:T(4,128)(2,1)S(1)}, u32[]{:S(2)}, u32[]{:S(2)}) async-start(bf16[32,4,1152]{2,1,0:T(4,128)(2,1)} %reshape.194), calls=%async_computation.1 | async-start | bytes 589824 | tf_op jit(solution)/shard_map/all_to_all | solution.py:643
  140.9 0.1 multiply_convert_fusion
  141.0 0.1 convert_element_type.166
  141.1 1.4 fusion.26
  142.6 0.2 reshape.202
  142.8 0.2 dot_general.72
  143.0 0.4 fusion.12
  143.4 7.9 %all-to-all-done.1 = bf16[32,4,1152]{2,1,0:T(4,128)(2,1)S(1)} async-done(((bf16[32,4,1152]{2,1,0:T(4,128)(2,1)}), bf16[32,4,1152]{2,1,0:T(4,128)(2,1)S(1)}, u32[]{:S(2)}, u32[]{:S(2)}) %all-to-all-start.1) | async-done | bytes 294944 | tf_op jit(solution)/shard_map/all_to_all | solution.py:643
  151.4 1.9 convolution_convert_fusion.9
  153.3 1.3 fusion.102
  154.7 0.8 convolution_bitcast_fusion
  155.5 7.8 %convolution_bitcast_fusion.1 = f32[256,8,72]{0,2,1:T(8,128)S(1)} fusion(bf16[128,8,72]{0,2,1:T(8,128)(2,1)S(1)} %bitcast.145, f32[8,128,256]{2,1,0:T(8,128)} %fusion.102, f32[8,128,256]{2,1,0:T(8,128)} %get-tuple-element.32, f32[8,128]{1,0:T(8,128)S(1)} %copy-done.31), kind=kOutput, calls=%fused_computation.27 | convolution fusion | flops 39585024 | bytes 2838528 | tf_op jit(solution)/shard_map/hqk,qhe->khe/dot_general | solution.py:548
  163.4 0.8 pad_maximum_fusion.3
  164.2 4.2 %collective-permute-start.1 = (bf16[128,1152]{0,1:T(8,128)(2,1)}, bf16[128,1152]{0,1:T(8,128)(2,1)}, u32[]{:S(2)}, u32[]{:S(2)}) collective-permute-start(bf16[128,1152]{0,1:T(8,128)(2,1)} %pad_maximum_fusion.3), channel_id=1, source_target_pairs={{0,1},{1,0},{2,3},{3,2},{4,5},{5,4},{6,7},{7,6},{8,9},{9,8},{10,11... | collective-permute-start | bytes 884744 | tf_op jit(solution)/shard_map/ppermute | solution.py:510
  168.4 1.6 convolution_convert_fusion.part
  170.0 45.7 %reduce_grads.1 = f32[18,1152]{1,0:T(8,128)} custom-call(bf16[576,1152]{1,0:T(8,128)(2,1)} %convolution_convert_fusion.part), custom_call_target="tpu_custom_call" | custom-call | bytes 8000000 | tf_op jit(solution)/shard_map/reduce_grads/pallas_call | solution.py:490
  215.7 0.8 reshape.192
  216.5 7.6 %convolution_convert_fusion.7 = bf16[8,72,128]{2,1,0:T(8,128)(2,1)S(1)} fusion(bf16[256,8,72]{0,2,1:T(8,128)(2,1)S(1)} %bitcast.137, f32[8,128,256]{2,1,0:T(8,128)} %fusion.102, f32[8,128,256]{2,1,0:T(8,128)} %get-tuple-element.32, f32[8,128]{1,0:T(8,128)S(1)} %copy-done.31), kind=kOutput, calls=%fused_computation.42 | convolution fusion | flops 39658752 | bytes 2543616 | tf_op jit(solution)/shard_map/hqk,khe->qhe/dot_general | solution.py:547
  224.2 1.0 convert_element_type.162
  225.3 3.7 %fusion.95 = (f32[128]{0:T(128)S(1)}, f32[128]{0:T(128)S(1)}, f32[128,1152]{1,0:T(8,128)S(1)}) fusion(f32[128]{0:T(128)S(1)} %copy-done.33, f32[128]{0:T(128)S(1)} %copy-done.29, bf16[1,1,128,1152]{3,2,1,0:T(8,128)(2,1)S(1)} %copy-done, f32[1152]{0:T(1024)S(1)} %copy-done.27, bf16[1152,1728]{1,0:T(8,128)(2,1)} %get-tuple-element.7, ...), kind=kOutput, calls=%fused_computation.146 | convolution fusion | flops 511966976 | bytes 5315072 | tf_op jit(solution)/shard_map/dot_general | solution.py:553
  229.1 1.0 fusion.59
  230.1 0.6 copy.64
  (91 shorter events, 0.6 us)
Async XLA Ops:
  1.5 78.6 %copy-start.26 = (f32[1152]{0:T(1024)}, f32[1152]{0:T(1024)S(1)}, u32[]{:S(2)}) copy-start(f32[1152]{0:T(1024)S(1)} %get-tuple-element.17) | copy-start | bytes 13828
  1.5 90.9 %copy-start.24 = (f32[1152]{0:T(1024)}, f32[1152]{0:T(1024)S(1)}, u32[]{:S(2)}) copy-start(f32[1152]{0:T(1024)S(1)} %get-tuple-element.18) | copy-start | bytes 13828
  1.5 98.6 %copy-start.21 = (f32[1152]{0:T(1024)}, f32[1152]{0:T(1024)S(1)}, u32[]{:S(2)}) copy-start(f32[1152]{0:T(1024)S(1)} %get-tuple-element.15) | copy-start | bytes 13828
  2.6 77.5 %copy-start.28 = (f32[128]{0:T(128)}, f32[128]{0:T(128)S(1)}, u32[]{:S(2)}) copy-start(f32[128]{0:T(128)S(1)} %broadcast_multiply_fusion.5) | copy-start | bytes 1540
  3.8 76.3 %copy-start.32 = (f32[128]{0:T(128)}, f32[128]{0:T(128)S(1)}, u32[]{:S(2)}) copy-start(f32[128]{0:T(128)S(1)} %add_rsqrt_fusion.1) | copy-start | bytes 1540
  80.1 9.7 %collective-permute-start = (bf16[128,1152]{0,1:T(8,128)(2,1)S(1)}, bf16[128,1152]{0,1:T(8,128)(2,1)S(1)}, u32[]{:S(2)}, u32[]{:S(2)}) collective-permute-start(bf16[128,1152]{0,1:T(8,128)(2,1)S(1)} %slice.97), channel_id=1, source_target_pairs={{0,1},{1,0},{2,3},{3,2},{4,5},{5,4},{6,7},{7,6},{8,9},{9,8},{10,11... | collective-permute-start | bytes 884744 | tf_op jit(solution)/shard_map/ppermute | solution.py:510
  83.8 7.7 %copy-start.15 = (bf16[128,576]{0,1:T(8,128)(2,1)}, bf16[128,576]{0,1:T(8,128)(2,1)S(1)}, u32[]{:S(2)}) copy-start(bf16[128,576]{0,1:T(8,128)(2,1)S(1)} %get-tuple-element.27) | copy-start | bytes 442372
  89.9 2.4 %copy-start.7 = (bf16[256,576]{0,1:T(8,128)(2,1)}, bf16[256,576]{0,1:T(8,128)(2,1)S(1)}, u32[]{:S(2)}) copy-start(bf16[256,576]{0,1:T(8,128)(2,1)S(1)} %get-tuple-element.38) | copy-start | bytes 884740
  89.9 2.4 %copy-start.10 = (bf16[256,576]{0,1:T(8,128)(2,1)}, bf16[256,576]{0,1:T(8,128)(2,1)S(1)}, u32[]{:S(2)}) copy-start(bf16[256,576]{0,1:T(8,128)(2,1)S(1)} %get-tuple-element.37) | copy-start | bytes 884740
  91.5 0.9 copy-start.30
  91.5 1.0 copy-start
  91.5 1.4 copy-start.2
  92.9 6.3 %copy-start.3 = (bf16[1,16,2,4,1152]{4,3,2,1,0:T(4,128)(2,1)S(1)}, bf16[1,16,2,4,1152]{4,3,2,1,0:T(4,128)(2,1)}, u32[]{:S(2)}) copy-start(bf16[1,16,2,4,1152]{4,3,2,1,0:T(4,128)(2,1)} %param.13) | copy-start | bytes 884740
  94.2 5.9 %copy-start.1 = (bf16[576,1152]{1,0:T(8,128)(2,1)S(1)}, bf16[576,1152]{1,0:T(8,128)(2,1)}, u32[]{:S(2)}) copy-start(bf16[576,1152]{1,0:T(8,128)(2,1)} %get-tuple-element.10) | copy-start | bytes 3981316
  94.2 16.4 %all-to-all-start = ((bf16[32,4,1152]{2,1,0:T(4,128)(2,1)}), bf16[32,4,1152]{2,1,0:T(4,128)(2,1)S(1)}, u32[]{:S(2)}, u32[]{:S(2)}) async-start(bf16[32,4,1152]{2,1,0:T(4,128)(2,1)} %reshape.190), calls=%async_computation | async-start | bytes 589824 | tf_op jit(solution)/shard_map/all_to_all | solution.py:589
  118.1 1.7 copy-start.12
  119.1 0.7 copy-start.13
  122.6 4.8 %copy-start.34 = (f32[8,8,16]{2,1,0:T(8,128)}, f32[8,8,16]{2,1,0:T(8,128)S(1)}, u32[]{:S(2)}) copy-start(f32[8,8,16]{2,1,0:T(8,128)S(1)} %get-tuple-element.33) | copy-start | bytes 12292
  122.6 2.5 %copy-start.18 = (bf16[16,8,1,8,72]{4,3,2,1,0:T(8,128)(2,1)S(1)}, bf16[16,8,1,8,72]{4,3,2,1,0:T(8,128)(2,1)}, u32[]{:S(2)}) copy-start(bf16[16,8,1,8,72]{4,3,2,1,0:T(8,128)(2,1)} %get-tuple-element.22) | copy-start | bytes 442372
  127.4 1.5 copy-start.19
  127.4 1.5 copy-start.20
  129.9 3.8 %copy-start.4 = (f32[16,8,1152]{2,1,0:T(8,128)S(1)}, f32[16,8,1152]{2,1,0:T(8,128)}, u32[]{:S(2)}) copy-start(f32[16,8,1152]{2,1,0:T(8,128)} %reshape.205) | copy-start | bytes 1769476
  133.7 7.2 %copy-start.22 = (f32[1152]{0:T(1024)S(1)}, f32[1152]{0:T(1024)}, u32[]{:S(2)}) copy-start(f32[1152]{0:T(1024)} %copy-done.21) | copy-start | bytes 13828
  134.0 7.1 %copy-start.14 = (bf16[16,8,1,8,72]{4,3,2,1,0:T(8,128)(2,1)S(1)}, bf16[16,8,1,8,72]{4,3,2,1,0:T(8,128)(2,1)}, u32[]{:S(2)}) copy-start(bf16[16,8,1,8,72]{4,3,2,1,0:T(8,128)(2,1)} %copy-done.13) | copy-start | bytes 442372
  134.8 16.5 %all-to-all-start.1 = ((bf16[32,4,1152]{2,1,0:T(4,128)(2,1)}), bf16[32,4,1152]{2,1,0:T(4,128)(2,1)S(1)}, u32[]{:S(2)}, u32[]{:S(2)}) async-start(bf16[32,4,1152]{2,1,0:T(4,128)(2,1)} %reshape.194), calls=%async_computation.1 | async-start | bytes 589824 | tf_op jit(solution)/shard_map/all_to_all | solution.py:643
  141.1 1.9 copy-start.23
  143.0 8.4 %copy-start.25 = (f32[1152]{0:T(1024)S(1)}, f32[1152]{0:T(1024)}, u32[]{:S(2)}) copy-start(f32[1152]{0:T(1024)} %copy-done.24) | copy-start | bytes 13828
  143.4 9.9 %copy-start.11 = (bf16[256,576]{0,1:T(8,128)(2,1)S(1)}, bf16[256,576]{0,1:T(8,128)(2,1)}, u32[]{:S(2)}) copy-start(bf16[256,576]{0,1:T(8,128)(2,1)} %copy-done.10) | copy-start | bytes 884740
  151.4 3.3 %copy-start.8 = (bf16[256,576]{0,1:T(8,128)(2,1)S(1)}, bf16[256,576]{0,1:T(8,128)(2,1)}, u32[]{:S(2)}) copy-start(bf16[256,576]{0,1:T(8,128)(2,1)} %copy-done.7) | copy-start | bytes 884740
  151.4 3.3 %copy-start.16 = (bf16[128,576]{0,1:T(8,128)(2,1)S(1)}, bf16[128,576]{0,1:T(8,128)(2,1)}, u32[]{:S(2)}) copy-start(bf16[128,576]{0,1:T(8,128)(2,1)} %copy-done.15) | copy-start | bytes 442372
  151.4 3.3 %copy-start.31 = (f32[8,128]{1,0:T(8,128)S(1)}, f32[8,128]{1,0:T(8,128)}, u32[]{:S(2)}) copy-start(f32[8,128]{1,0:T(8,128)} %copy-done.30) | copy-start | bytes 12292
  155.5 61.0 %copy-start.6 = (f32[256,8,72]{0,2,1:T(8,128)}, f32[256,8,72]{0,2,1:T(8,128)S(1)}, u32[]{:S(2)}) copy-start(f32[256,8,72]{0,2,1:T(8,128)S(1)} %convolution_bitcast_fusion) | copy-start | bytes 1769476
  163.3 53.1 %copy-start.5 = (f32[256,8,72]{0,2,1:T(8,128)}, f32[256,8,72]{0,2,1:T(8,128)S(1)}, u32[]{:S(2)}) copy-start(f32[256,8,72]{0,2,1:T(8,128)S(1)} %convolution_bitcast_fusion.1) | copy-start | bytes 1769476
  164.2 60.0 %collective-permute-start.1 = (bf16[128,1152]{0,1:T(8,128)(2,1)}, bf16[128,1152]{0,1:T(8,128)(2,1)}, u32[]{:S(2)}, u32[]{:S(2)}) collective-permute-start(bf16[128,1152]{0,1:T(8,128)(2,1)} %pad_maximum_fusion.3), channel_id=1, source_target_pairs={{0,1},{1,0},{2,3},{3,2},{4,5},{5,4},{6,7},{7,6},{8,9},{9,8},{10,11... | collective-permute-start | bytes 884744 | tf_op jit(solution)/shard_map/ppermute | solution.py:510
  170.0 46.5 %copy-start.9 = (bf16[256,576]{0,1:T(8,128)(2,1)S(1)}, bf16[256,576]{0,1:T(8,128)(2,1)}, u32[]{:S(2)}) copy-start(bf16[256,576]{0,1:T(8,128)(2,1)} %copy-done.7) | copy-start | bytes 884740
  216.5 8.7 %slice-start = ((f32[256,8,72]{0,2,1:T(8,128)}), f32[128,8,72]{0,2,1:T(8,128)S(1)}, s32[]{:S(2)}) async-start(f32[256,8,72]{0,2,1:T(8,128)} %copy-done.5), calls=%async_computation.2 | async-start | bytes 589824 | tf_op jit(solution)/shard_map/slice | solution.py:670
  216.5 8.7 %slice-start.1 = ((f32[256,8,72]{0,2,1:T(8,128)}), f32[128,8,72]{0,2,1:T(8,128)S(1)}, s32[]{:S(2)}) async-start(f32[256,8,72]{0,2,1:T(8,128)} %copy-done.6), calls=%async_computation.3 | async-start | bytes 589824 | tf_op jit(solution)/shard_map/slice | solution.py:673
  224.1 1.1 copy-start.27
  224.2 1.1 copy-start.29
  224.2 1.1 copy-start.33
  229.1 1.1 copy-start.17

commit v2 on v1

v2 whole, which is shorter than its diff:
```python
import jax
import jax.numpy as jnp
from jax import lax
from jax.experimental import pallas as pl
from jax.experimental.pallas import tpu as pltpu
from jax.sharding import PartitionSpec as P

HEAD_DIM = 72
MESH = pl.DeviceIdType.MESH
LOW, RING = 4, 8
TILE = (16, 128)


class Place:
    def __init__(self):
        outer = lax.axis_index("dp")
        inner = lax.axis_index("seq")
        self.core = lax.rem(outer, 2)
        self.high = lax.rem(lax.div(outer, 2), 2)
        self.x = lax.div(outer, 4)
        self.low = lax.div(inner, RING)
        self.y = lax.rem(inner, RING)
        self.z = self.high * LOW + self.low
        self.way = 1 - 2 * self.core

    def low_at(self, step):
        return lax.rem(self.low + step + LOW, LOW)

    def y_at(self, step):
        return lax.rem(self.y + step + RING, RING)

    def device(self, x=None, y=None, z=None, core=None):
        x = self.x if x is None else x
        y = self.y if y is None else y
        z = self.z if z is None else z
        core = self.core if core is None else core
        outer = (x * 2 + lax.div(z, LOW)) * 2 + core
        return (outer, lax.rem(z, LOW) * RING + y)

    def y_to(self, step):
        return self.device(y=self.y_at(step))

    def z_to(self, step):
        return self.device(z=lax.rem(self.z + step + RING, RING))

    def sibling(self):
        return self.device(core=1 - self.core)


def greet(devices):
    barrier = pltpu.get_barrier_semaphore()
    for device in devices:
        pl.semaphore_signal(barrier, inc=1, device_id=device, device_id_type=MESH)
    return len(devices)


class Link:
    def __init__(self, send_sems, recv_sems):
        self.send_sems, self.recv_sems = send_sems, recv_sems
        self.count = 0
        self.started = []

    def number(self):
        self.count += 1
        return self.count - 1

    def copy(self, number, source, target, device):
        return pltpu.make_async_remote_copy(
            src_ref=source,
            dst_ref=target,
            send_sem=self.send_sems.at[number],
            recv_sem=self.recv_sems.at[number],
            device_id=device,
            device_id_type=MESH,
        )

    def send(self, source, target, device):
        number = self.number()
        copy = self.copy(number, source, target, device)
        copy.start()
        self.started.append(copy)
        return number

    def arrived(self, number, target, device):
        self.copy(number, target, target, device).wait_recv()

    def finish(self):
        for copy in self.started:
            copy.wait_send()
        self.started = []


def gather_y_first(place, link, held, first, other, count):
    way = place.way
    up, down = place.y_to(1), place.y_to(-1)
    above, below = place.z_to(1), place.z_to(-1)
    sibling = place.sibling()

    def one(step):
        return held.at[place.low, place.y_at(step), pl.ds(first, count)]

    def ring(step, start):
        return held.at[place.low_at(step), :, pl.ds(start, count)]

    def go(ref, device):
        return link.send(ref, ref, device)

    plus, minus = go(one(0), up), go(one(0), down)
    yield
    for step in (1, 2):
        link.arrived(plus, one(-step), up)
        plus = go(one(-step), up)
        link.arrived(minus, one(step), down)
        minus = go(one(step), down)
        yield
    link.arrived(plus, one(-3), up)
    link.arrived(minus, one(3), down)
    last = go(one(-3 * way), place.y_to(way))
    yield
    link.arrived(last, one(4), up)
    plus, minus = go(ring(0, first), above), go(ring(0, first), below)
    shared = [(go(ring(0, first), sibling), 0)]
    yield
    link.arrived(plus, ring(-1, first), above)
    link.arrived(minus, ring(1, first), below)
    last = go(ring(-way, first), place.z_to(way))
    shared.append((go(ring(-1, first), sibling), -1))
    shared.append((go(ring(1, first), sibling), 1))
    yield
    link.arrived(last, ring(2, first), above)
    shared.append((go(ring(2, first), sibling), 2))
    yield
    for number, step in shared:
        link.arrived(number, ring(step, other), sibling)
    yield


def gather_z_first(place, link, held, first, other, count):
    way = place.way
    up, down = place.y_to(1), place.y_to(-1)
    above, below = place.z_to(1), place.z_to(-1)
    sibling = place.sibling()

    def one(step):
        return held.at[place.low_at(step), place.y, pl.ds(first, count)]

    def run(step, start):
        return held.at[:, place.y_at(step), pl.ds(start, count)]

    def go(ref, device):
        return link.send(ref, ref, device)

    plus, minus = go(one(0), above), go(one(0), below)
    yield
    link.arrived(plus, one(-1), above)
    link.arrived(minus, one(1), below)
    last = go(one(-way), place.z_to(way))
    yield
    link.arrived(last, one(2), above)
    plus, minus = go(run(0, first), up), go(run(0, first), down)
    shared = [(go(run(0, first), sibling), 0)]
    yield
    for step in (1, 2):
        link.arrived(plus, run(-step, first), up)
        plus = go(run(-step, first), up)
        link.arrived(minus, run(step, first), down)
        minus = go(run(step, first), down)
        shared.append((go(run(-step, first), sibling), -step))
        shared.append((go(run(step, first), sibling), step))
        yield
    link.arrived(plus, run(-3, first), up)
    link.arrived(minus, run(3, first), down)
    last = go(run(-3 * way, first), place.y_to(way))
    shared.append((go(run(-3, first), sibling), -3))
    shared.append((go(run(3, first), sibling), 3))
    yield
    link.arrived(last, run(4, first), up)
    shared.append((go(run(4, first), sibling), 4))
    yield
    for number, step in shared:
        link.arrived(number, run(step, other), sibling)
    yield


def gather(place, link, held, begin, y_count, z_count):
    half = y_count + z_count
    mine, other = begin + place.core * half, begin + (1 - place.core) * half
    plans = [
        gather_y_first(place, link, held, mine, other, y_count),
        gather_z_first(place, link, held, mine + y_count, other + y_count, z_count),
    ]
    while plans:
        for plan in list(plans):
            if next(plan, plans) is plans:
                plans.remove(plan)
        yield


def lane_tiles(width):
    return [(at, min(128, width - at)) for at in range(0, width, 128)]


def pack_own(shard, staged, wide, local, begin):
    rows, width = shard.shape
    full, rest = rows // 16, rows % 16
    tiles = lane_tiles(width)
    number = begin
    for block in range(full):
        for at, lanes in tiles:
            local[number, :, :lanes] = shard[16 * block : 16 * block + 16, at : at + lanes]
            number += 1
    per = 16 // rest
    wide[:rest, :width] = shard[16 * full :, :].astype(jnp.float32)
    groups = -(-len(tiles) // per)
    for index, (at, lanes) in enumerate(tiles):
        staged[index // per, pl.ds(rest * (index % per), rest), :lanes] = wide[
            :rest, at : at + lanes
        ]
    for group in range(groups):
        local[number + group] = staged[group].astype(jnp.bfloat16)


def hold_own(place, local, held, begin, count):
    mine = pl.ds(begin + place.core * (count // 2), count // 2)
    held[place.low, place.y, mine] = local[mine]


def unpack_all(held, begin, rows, width, stage, out):
    full, rest = rows // 16, rows % 16
    tiles = lane_tiles(width)
    per = 16 // rest
    several = 4 if rows == 36 else 8
    block = several * rows

    def step(index, carry):
        low, y = lax.div(index * several, RING), lax.rem(index * several, RING)
        for shard in range(several):
            top = shard * rows
            for part in range(full):
                for tile, (at, lanes) in enumerate(tiles):
                    value = held[low, y + shard, begin + part * len(tiles) + tile]
                    stage[top + 16 * part : top + 16 * part + 16, at : at + lanes] = value.astype(
                        jnp.float32
                    )[:, :lanes]
            for group in range(-(-len(tiles) // per)):
                value = held[low, y + shard, begin + full * len(tiles) + group]
                value = value.astype(jnp.float32)
                for piece in range(per):
                    tile = group * per + piece
                    if tile < len(tiles):
                        at, lanes = tiles[tile]
                        stage[top + 16 * full : top + rows, at : at + lanes] = value[
                            rest * piece : rest * piece + rest, :lanes
                        ]
        out[pl.ds(pl.multiple_of(index * block, 16), block), :] = stage[:block, :width].astype(
            jnp.bfloat16
        )
        return carry

    lax.fori_loop(0, 32 // several, step, 0)


PROJECT_TILES, MERGE_TILES = 32, 12
HELD_TILES = 2 * (PROJECT_TILES + MERGE_TILES)
GATHER_COPIES = 32
REDUCE_COPIES = 16


def reduce_plan(place, link, packed, near, total, long_out, long_in, short_out, short_in, small, final):
    way, half = place.way, MERGE_TILES // 2
    mine, other = place.core * half, (1 - place.core) * half
    sibling = place.sibling()
    number = link.send(packed.at[:, :, pl.ds(other, half)], near, sibling)
    yield
    link.arrived(number, near, sibling)

    def add(low, carry):
        for y in range(RING):
            total[low, y] = packed[low, y, pl.ds(mine, half)].astype(jnp.float32) + near[
                low, y
            ].astype(jnp.float32)
        return carry

    lax.fori_loop(0, LOW, add, 0)
    there, back = place.y_to(way), place.y_to(-way)
    for step in range(4):
        value = total[:, place.y_at((4 - step) * way)]
        if step:
            link.arrived(long_number, long_in.at[step - 1], there)
            value = value + long_in[step - 1].astype(jnp.float32)
        long_out[step] = value.astype(jnp.bfloat16)
        long_number = link.send(long_out.at[step], long_in.at[step], there)
        if step < 3:
            value = total[:, place.y_at((step - 3) * way)]
            if step:
                link.arrived(short_number, short_in.at[step - 1], back)
                value = value + short_in[step - 1].astype(jnp.float32)
            short_out[step] = value.astype(jnp.bfloat16)
            short_number = link.send(short_out.at[step], short_in.at[step], back)
        yield
    link.arrived(short_number, short_in.at[2], back)
    link.arrived(long_number, long_in.at[3], there)
    small[pl.ds(0, 4)] = (
        total[:, place.y] + long_in[3].astype(jnp.float32) + short_in[2].astype(jnp.float32)
    )
    parity, upper = lax.rem(place.low, 2), lax.div(place.low, 2)
    device = place.device(z=place.z + 1 - 2 * parity)
    numbers = [
        link.send(small.at[1 - parity + 2 * k], small.at[4 + k], device) for k in range(2)
    ]
    yield
    for k in range(2):
        link.arrived(numbers[k], small.at[4 + k], device)
        small[6 + k] = small[parity + 2 * k] + small[4 + k]
    device = place.device(z=place.z + 2 - 4 * upper)
    number = link.send(small.at[7 - upper], small.at[8], device)
    yield
    link.arrived(number, small.at[8], device)
    small[9] = small[6 + upper] + small[8]
    at = 9
    for device in (
        place.device(z=lax.rem(place.z + LOW, RING)),
        place.device(x=place.x + 1 - 2 * lax.rem(place.x, 2)),
        place.device(x=lax.rem(place.x + 2, 4)),
    ):
        number = link.send(small.at[at], small.at[at + 1], device)
        yield
        link.arrived(number, small.at[at + 1], device)
        small[at + 2] = small[at] + small[at + 1]
        at += 2
    final[pl.ds(mine, half)] = small[at]
    number = link.send(final.at[pl.ds(mine, half)], final.at[pl.ds(mine, half)], sibling)
    yield
    link.arrived(number, final.at[pl.ds(other, half)], sibling)


def pack_partial(part, stage, staged, packed):
    def step(low, carry):
        stage[...] = part[pl.ds(pl.multiple_of(low * 144, 16), 144), :].astype(jnp.float32)
        staged[...] = jnp.zeros_like(staged)
        for y in range(RING):
            for tile in range(9):
                at = 128 * tile
                packed[low, y, tile] = stage[18 * y : 18 * y + 16, at : at + 128].astype(
                    jnp.bfloat16
                )
                staged[y, tile // 8, 2 * (tile % 8) : 2 * (tile % 8) + 2, :] = stage[
                    18 * y + 16 : 18 * y + 18, at : at + 128
                ]
            for group in range(3):
                packed[low, y, 9 + group] = staged[y, group].astype(jnp.bfloat16)
        return carry

    lax.fori_loop(0, LOW, step, 0)


def unpack_final(final, out):
    for tile in range(9):
        at = 128 * tile
        out[0:16, at : at + 128] = final[tile]
        out[16:18, at : at + 128] = final[9 + tile // 8, 2 * (tile % 8) : 2 * (tile % 8) + 2, :]


MEMBERS, TOKENS, MODEL, INNER, HEADS = 32, 128, 1152, 576, 8
EPSILON = 1e-06
FACTOR = HEAD_DIM ** (-0.5)


def dot(left, right):
    return jnp.dot(left, right, preferred_element_type=jnp.float32)


def dot_lanes(left, right):
    return lax.dot_general(left, right, (((1,), (1,)), ((), ())), preferred_element_type=jnp.float32)


def dot_rows(left, right):
    return lax.dot_general(left, right, (((0,), (0,)), ((), ())), preferred_element_type=jnp.float32)


def normalize(widened):
    average = jnp.mean(widened, -1, keepdims=True)
    centered = widened - average
    variance = jnp.mean(centered * centered, -1, keepdims=True)
    inverse_std = lax.rsqrt(variance + EPSILON)
    return (centered * inverse_std, inverse_std)


def modulate_back(grad_modulated, normed, inverse_std, scale_row):
    grad_normed = grad_modulated * (1.0 + scale_row)
    first_mean = jnp.mean(grad_normed, -1, keepdims=True)
    second_mean = jnp.mean(grad_normed * normed, -1, keepdims=True)
    return inverse_std * (grad_normed - first_mean - normed * second_mean)


def head_windows():
    for head in range(HEADS):
        first = HEAD_DIM * head
        start, stop = first // 128 * 128, min(INNER, -(-(first + HEAD_DIM) // 128) * 128)
        lane = lax.broadcasted_iota(jnp.int32, (1, stop - start), 1) + start
        inside = jnp.logical_and(lane >= first, lane < first + HEAD_DIM)
        yield head, slice(start, stop), jnp.where(inside, 1.0, 0.0).astype(jnp.bfloat16)


def attend(queries, keys, values, probs_ref, attended, allowed=None):
    attended[...] = jnp.zeros_like(attended)
    for head, window, own in head_windows():
        scores = dot_lanes(queries[:, window] * own, keys[:, window]) * FACTOR
        if allowed is not None:
            scores = jnp.where(allowed, scores, -1e30)
        raised = jnp.exp(scores - jnp.max(scores, -1, keepdims=True))
        probs = raised * (1.0 / jnp.sum(raised, -1, keepdims=True))
        probs_ref[head] = probs
        attended[:, window] += dot(probs.astype(jnp.bfloat16), values[:, window] * own)


def score_grads(grad_attended, own, window, values, probs):
    grad_probs = dot_lanes(grad_attended[:, window] * own, values[:, window])
    totals = jnp.sum(probs * grad_probs, -1, keepdims=True)
    return (probs * (grad_probs - totals) * FACTOR).astype(jnp.bfloat16)


def from_blocks(blocks, wide):
    def step(pair, carry):
        rows = pl.ds(pl.multiple_of(8 * pair, 8), 8)
        wide[rows, :] = jnp.concatenate(
            [blocks[2 * pair].astype(jnp.float32), blocks[2 * pair + 1].astype(jnp.float32)], 0
        )
        return carry

    lax.fori_loop(0, MEMBERS // 2, step, 0)


def to_blocks(wide, blocks):
    def step(pair, carry):
        value = wide[pl.ds(pl.multiple_of(8 * pair, 8), 8), :]
        blocks[2 * pair] = value[:4].astype(jnp.bfloat16)
        blocks[2 * pair + 1] = value[4:].astype(jnp.bfloat16)
        return carry

    lax.fori_loop(0, MEMBERS // 2, step, 0)


def block_copy(away, source, target, sent, come, device):
    return pltpu.make_async_remote_copy(
        src_ref=source,
        dst_ref=target,
        send_sem=sent.at[away],
        recv_sem=come.at[away],
        device_id=device,
        device_id_type=MESH,
    )


def trade_start(leaving, coming, sent, come):
    outer, me = lax.axis_index("dp"), lax.axis_index("seq")

    def step(away, carry):
        there = lax.rem(me + away, MEMBERS)
        block_copy(
            away, leaving.at[there], coming.at[me], sent, come, (outer, there)
        ).start()
        return carry

    lax.fori_loop(1, MEMBERS, step, 0)
    coming[me] = leaving[me]


def trade_wait(leaving, coming, sent, come):
    outer, me = lax.axis_index("dp"), lax.axis_index("seq")

    def step(away, carry):
        there = lax.rem(me + away, MEMBERS)
        origin = lax.rem(me + MEMBERS - away, MEMBERS)
        block_copy(
            away, leaving.at[there], coming.at[origin], sent, come, (outer, there)
        ).wait()
        return carry

    lax.fori_loop(1, MEMBERS, step, 0)


def partners(place):
    outer = lax.axis_index("dp")
    me = lax.axis_index("seq")
    listed = [(outer, lax.rem(me + away, MEMBERS)) for away in range(1, MEMBERS)]
    return listed + [
        place.sibling(),
        place.z_to(1),
        place.z_to(-1),
        place.z_to(LOW),
        place.device(x=place.x + 1 - 2 * lax.rem(place.x, 2)),
        place.device(x=lax.rem(place.x + 2, 4)),
    ]


def advance(plans, rounds=1000):
    for _ in range(rounds):
        for plan in list(plans):
            if next(plan, plans) is plans:
                plans.remove(plan)
        if not plans:
            return


def split_packed(packed, rows, queries, keys, values):
    queries[...] = packed[:TOKENS, :INNER].astype(jnp.bfloat16)
    keys[...] = packed[:rows, INNER : 2 * INNER].astype(jnp.bfloat16)
    values[...] = packed[:rows, 2 * INNER : 3 * INNER].astype(jnp.bfloat16)


def scratch_table():
    f32, b16 = jnp.float32, jnp.bfloat16
    half = MERGE_TILES // 2
    project, merge = (MODEL, 3 * INNER), (INNER, MODEL)
    wide, narrow = (TOKENS, MODEL), (TOKENS, INNER)
    blocks = (MEMBERS, 4, MODEL)
    sems = pltpu.SemaphoreType.DMA
    return {
        "held": pltpu.VMEM((LOW, RING, HELD_TILES) + TILE, b16),
        "local": pltpu.VMEM((HELD_TILES,) + TILE, b16),
        "staged": pltpu.VMEM((4,) + TILE, f32),
        "loose": pltpu.VMEM((8, 1792), f32),
        "stage": pltpu.VMEM((144, 1792), f32),
        "space_project": pltpu.VMEM(project, b16),
        "space_merge": pltpu.VMEM(merge, b16),
        "time_project": pltpu.VMEM(project, b16),
        "time_merge": pltpu.VMEM(merge, b16),
        "gather_sent": sems((3, GATHER_COPIES)),
        "gather_come": sems((3, GATHER_COPIES)),
        "reduce_stage": pltpu.VMEM((144, MODEL), f32),
        "reduce_staged": pltpu.VMEM((RING, 3) + TILE, f32),
        "part": pltpu.VMEM(merge, f32),
        "packed_part": pltpu.VMEM((LOW, RING, MERGE_TILES) + TILE, b16),
        "near": pltpu.VMEM((LOW, RING, half) + TILE, b16),
        "total": pltpu.VMEM((LOW, RING, half) + TILE, f32),
        "long_out": pltpu.VMEM((4, LOW, half) + TILE, b16),
        "long_in": pltpu.VMEM((4, LOW, half) + TILE, b16),
        "short_out": pltpu.VMEM((3, LOW, half) + TILE, b16),
        "short_in": pltpu.VMEM((3, LOW, half) + TILE, b16),
        "small": pltpu.VMEM((16, half) + TILE, f32),
        "final": pltpu.VMEM((MERGE_TILES,) + TILE, f32),
        "reduce_sent": sems((REDUCE_COPIES,)),
        "reduce_come": sems((REDUCE_COPIES,)),
        "both_tokens": pltpu.VMEM((2,) + wide, b16),
        "modulated": pltpu.VMEM((2 * TOKENS, MODEL), b16),
        "packed": pltpu.VMEM((2 * TOKENS, 1792), f32),
        "space_normed": pltpu.VMEM(wide, f32),
        "space_inverse": pltpu.VMEM((TOKENS, 1), f32),
        "space_queries": pltpu.VMEM(narrow, b16),
        "space_keys": pltpu.VMEM((2 * TOKENS, INNER), b16),
        "space_values": pltpu.VMEM((2 * TOKENS, INNER), b16),
        "space_probs": pltpu.VMEM((HEADS, TOKENS, 2 * TOKENS), f32),
        "attended": pltpu.VMEM(narrow, f32),
        "time_normed": pltpu.VMEM(wide, f32),
        "time_queries": pltpu.VMEM(narrow, b16),
        "time_keys": pltpu.VMEM(narrow, b16),
        "time_values": pltpu.VMEM(narrow, b16),
        "time_probs": pltpu.VMEM((HEADS, TOKENS, TOKENS), f32),
        "wide": pltpu.VMEM(wide, f32),
        "across": pltpu.VMEM(wide, f32),
        "grad_result": pltpu.VMEM(wide, f32),
        "grad_attended": pltpu.VMEM(narrow, b16),
        "grad_scores": pltpu.VMEM((HEADS, TOKENS, 2 * TOKENS), b16),
        "grad_queries": pltpu.VMEM(narrow, f32),
        "grad_keys": pltpu.VMEM((2 * TOKENS, INNER), f32),
        "grad_values": pltpu.VMEM((2 * TOKENS, INNER), f32),
        "grad_packed": pltpu.VMEM((TOKENS, 1792), f32),
        "far_out": pltpu.VMEM((2,) + narrow, b16),
        "far_in": pltpu.VMEM((2,) + narrow, b16),
        "middle_out": pltpu.VMEM(blocks, b16),
        "middle_in": pltpu.VMEM(blocks, b16),
        "grad_out": pltpu.VMEM(blocks, b16),
        "grad_in": pltpu.VMEM(blocks, b16),
        "middle_sent": sems((MEMBERS,)),
        "middle_come": sems((MEMBERS,)),
        "grad_sent": sems((MEMBERS,)),
        "grad_come": sems((MEMBERS,)),
        "pair_sent": sems((2,)),
        "pair_come": sems((2,)),
    }


class Refs:
    def __init__(self, refs):
        for name, ref in zip(scratch_table(), refs, strict=True):
            setattr(self, name, ref)


def join_packed(grad_packed, queries, keys, values):
    grad_packed[:, :INNER] = queries
    grad_packed[:, INNER : 2 * INNER] = keys
    grad_packed[:, 2 * INNER : 3 * INNER] = values
    return grad_packed[:, : 3 * INNER].astype(jnp.bfloat16)


def clip_kernel(
    tokens,
    modulation,
    space_project,
    space_merge,
    time_project,
    time_merge,
    cotangent,
    result,
    token_grads,
    merge_grads,
    *scratch,
):
    at = Refs(scratch)
    place = Place()
    expected = greet(partners(place))

    def row(index):
        return modulation[index : index + 1, :]

    starts = (0, PROJECT_TILES, PROJECT_TILES + MERGE_TILES, 2 * PROJECT_TILES + MERGE_TILES)
    for shard, start in zip((space_project, space_merge, time_project, time_merge), starts):
        pack_own(shard, at.staged, at.loose, at.local, start)
    hold_own(place, at.local, at.held, 0, 32)
    hold_own(place, at.local, at.held, starts[1], 12)
    hold_own(place, at.local, at.held, starts[2], 44)
    at.both_tokens[0] = tokens[...]
    links = [Link(at.gather_sent.at[i], at.gather_come.at[i]) for i in range(3)]
    first = [gather(place, links[0], at.held, 0, 9, 7)]
    later = [
        gather(place, links[1], at.held, starts[1], 4, 2),
        gather(place, links[2], at.held, starts[2], 13, 9),
    ]
    pl.semaphore_wait(pltpu.get_barrier_semaphore(), expected)
    advance(first, 1)
    pair = Link(at.pair_sent, at.pair_come)
    partner = place.y_to(1 - 2 * lax.rem(place.y, 2))
    number = pair.send(at.both_tokens.at[0], at.both_tokens.at[1], partner)
    advance(first, 1)
    advance(later, 1)
    normed, inverse_std = normalize(tokens[...].astype(jnp.float32))
    at.space_normed[...] = normed
    at.space_inverse[...] = inverse_std
    at.modulated[:TOKENS] = (normed * (1.0 + row(1)) + row(0)).astype(jnp.bfloat16)
    from_blocks(cotangent, at.grad_result)
    advance(first, 1)
    pair.arrived(number, at.both_tokens.at[1], partner)
    normed, _ = normalize(at.both_tokens[1].astype(jnp.float32))
    at.modulated[TOKENS:] = (normed * (1.0 + row(1)) + row(0)).astype(jnp.bfloat16)
    while first:
        advance(first, 1)
        advance(later, 1)
    unpack_all(at.held, starts[0], 36, 1728, at.stage, at.space_project)

    at.packed[:, : 3 * INNER] = dot(at.modulated[...], at.space_project[...])
    split_packed(at.packed, 2 * TOKENS, at.space_queries, at.space_keys, at.space_values)
    advance(later, 1)
    attend(at.space_queries, at.space_keys, at.space_values, at.space_probs, at.attended)
    advance(later)
    unpack_all(at.held, starts[1], 18, 1152, at.stage, at.space_merge)
    branch = dot(at.attended[...].astype(jnp.bfloat16), at.space_merge[...])
    at.wide[...] = tokens[...].astype(jnp.float32) + row(2) * branch
    to_blocks(at.wide, at.middle_out)
    trade_start(at.middle_out, at.middle_in, at.middle_sent, at.middle_come)
    unpack_all(at.held, starts[2], 36, 1728, at.stage, at.time_project)
    unpack_all(at.held, starts[3], 18, 1152, at.stage, at.time_merge)
    scaled = (row(5) * at.grad_result[...]).astype(jnp.bfloat16)
    at.grad_attended[...] = dot_lanes(scaled, at.time_merge[...]).astype(jnp.bfloat16)
    trade_wait(at.middle_out, at.middle_in, at.middle_sent, at.middle_come)
    from_blocks(at.middle_in, at.across)

    normed, time_inverse = normalize(at.across[...])
    at.time_normed[...] = normed
    modulated = (normed * (1.0 + row(4)) + row(3)).astype(jnp.bfloat16)
    at.packed[:TOKENS, : 3 * INNER] = dot(modulated, at.time_project[...])
    split_packed(at.packed, TOKENS, at.time_queries, at.time_keys, at.time_values)
    square = (TOKENS, TOKENS)
    patch_row = lax.rem(lax.broadcasted_iota(jnp.int32, square, 0), 8)
    patch_column = lax.rem(lax.broadcasted_iota(jnp.int32, square, 1), 8)
    attend(
        at.time_queries,
        at.time_keys,
        at.time_values,
        at.time_probs,
        at.attended,
        patch_row == patch_column,
    )
    flat = at.attended[...].astype(jnp.bfloat16)
    scaled = (row(5) * at.grad_result[...]).astype(jnp.bfloat16)
    at.part[...] = dot_rows(flat, scaled)
    pack_partial(at.part, at.reduce_stage, at.reduce_staged, at.packed_part)
    reducing = Link(at.reduce_sent, at.reduce_come)
    reduction = [
        reduce_plan(
            place, reducing, at.packed_part, at.near, at.total, at.long_out, at.long_in,
            at.short_out, at.short_in, at.small, at.final,
        )
    ]
    advance(reduction, 1)
    at.wide[...] = at.across[...] + row(5) * dot(flat, at.time_merge[...])
    to_blocks(at.wide, result)
    advance(reduction, 1)

    at.grad_queries[...] = jnp.zeros_like(at.grad_queries)
    at.grad_keys[...] = jnp.zeros_like(at.grad_keys)
    at.grad_values[...] = jnp.zeros_like(at.grad_values)
    for head, window, own in head_windows():
        probs = at.time_probs[head]
        grads = score_grads(at.grad_attended, own, window, at.time_values, probs)
        at.grad_values[:TOKENS, window] += dot_rows(
            probs.astype(jnp.bfloat16), at.grad_attended[:, window] * own
        )
        at.grad_keys[:TOKENS, window] += dot_rows(grads, at.time_queries[:, window] * own)
        at.grad_queries[:, window] += dot(grads, at.time_keys[:, window] * own)
    grad_packed = join_packed(
        at.grad_packed, at.grad_queries[...], at.grad_keys[:TOKENS], at.grad_values[:TOKENS]
    )
    grad_modulated = dot_lanes(grad_packed, at.time_project[...])
    at.wide[...] = at.grad_result[...] + modulate_back(
        grad_modulated, at.time_normed[...], time_inverse, row(4)
    )
    to_blocks(at.wide, at.grad_out)
    trade_start(at.grad_out, at.grad_in, at.grad_sent, at.grad_come)
    advance(reduction, 2)
    trade_wait(at.grad_out, at.grad_in, at.grad_sent, at.grad_come)
    from_blocks(at.grad_in, at.wide)

    scaled = (row(2) * at.wide[...]).astype(jnp.bfloat16)
    at.grad_attended[...] = dot_lanes(scaled, at.space_merge[...]).astype(jnp.bfloat16)
    at.grad_keys[...] = jnp.zeros_like(at.grad_keys)
    at.grad_values[...] = jnp.zeros_like(at.grad_values)
    at.grad_queries[...] = jnp.zeros_like(at.grad_queries)
    far = pl.ds(TOKENS, TOKENS)
    for head, window, own in head_windows():
        probs = at.space_probs[head]
        grads = score_grads(at.grad_attended, own, window, at.space_values, probs)
        at.grad_scores[head] = grads
        at.grad_values[:, window] += dot_rows(
            probs.astype(jnp.bfloat16), at.grad_attended[:, window] * own
        )
        at.grad_keys[:, window] += dot_rows(grads, at.space_queries[:, window] * own)
    at.far_out[0] = at.grad_keys[far, :].astype(jnp.bfloat16)
    at.far_out[1] = at.grad_values[far, :].astype(jnp.bfloat16)
    number = pair.send(at.far_out, at.far_in, partner)
    advance(reduction, 1)
    for head, window, own in head_windows():
        at.grad_queries[:, window] += dot(at.grad_scores[head], at.space_keys[:, window] * own)
    advance(reduction, 1)
    pair.arrived(number, at.far_in, partner)
    grad_packed = join_packed(
        at.grad_packed,
        at.grad_queries[...],
        at.grad_keys[:TOKENS] + at.far_in[0].astype(jnp.float32),
        at.grad_values[:TOKENS] + at.far_in[1].astype(jnp.float32),
    )
    advance(reduction, 1)
    grad_modulated = dot_lanes(grad_packed, at.space_project[...])
    token_grads[...] = (
        at.wide[...]
        + modulate_back(grad_modulated, at.space_normed[...], at.space_inverse[...], row(1))
    ).astype(jnp.bfloat16)
    advance(reduction)
    unpack_final(at.final, merge_grads)
    for link in links + [pair, reducing]:
        link.finish()


def body(
    tokens, modulation, spatial_project, spatial_merge, temporal_project, temporal_merge, cotangent
):
    vmem = pl.BlockSpec(memory_space=pltpu.VMEM)
    blocks = (MEMBERS, 4, MODEL)
    result, token_grads, merge_grads = pl.pallas_call(
        clip_kernel,
        out_shape=[
            jax.ShapeDtypeStruct(blocks, jnp.bfloat16),
            jax.ShapeDtypeStruct((TOKENS, MODEL), jnp.bfloat16),
            jax.ShapeDtypeStruct((18, MODEL), jnp.float32),
        ],
        in_specs=[vmem] * 7,
        out_specs=[vmem] * 3,
        scratch_shapes=list(scratch_table().values()),
        compiler_params=pltpu.CompilerParams(
            collective_id=0, has_side_effects=True, vmem_limit_bytes=60 * 1024 * 1024
        ),
        cost_estimate=pl.CostEstimate(
            flops=3_000_000_000, bytes_accessed=4_000_000, transcendentals=500_000
        ),
        name="clip_step",
    )(
        tokens.reshape(TOKENS, MODEL),
        modulation.reshape(6, MODEL),
        spatial_project,
        spatial_merge,
        temporal_project,
        temporal_merge,
        cotangent.reshape(blocks),
    )
    return (
        result.reshape(1, 16, 2, 4, MODEL),
        token_grads.reshape(1, 1, TOKENS, MODEL),
        merge_grads,
    )


def solution(mesh):
    in_specs = (
        P("dp", "seq", None, None),
        P("dp", None, None),
        P("seq", None),
        P("seq", None),
        P("seq", None),
        P("seq", None),
        P("dp", None, None, "seq", None),
    )
    out_specs = (P("dp", None, None, "seq", None), P("dp", "seq", None, None), P("seq", None))
    return jax.shard_map(body, mesh=mesh, in_specs=in_specs, out_specs=out_specs, check_vma=False)
```

time: 232 us -> 153 us (0.66)
  the two profiles are of different devices: /device:TPU:1 before, /device:TPU:9 now
where the time goes in v2:
time: 153 us
  Pallas kernels  147 us (96%)
  local copies, waits for them, and re-layouts  4.83 us (3%)
    pallas_call x1, Pallas kernels, body(): pl.pallas_call(clip_kernel, out_shape=[jax.ShapeDtypeStruct(blocks, jnp.b...  147 us
    unnamed x8, local copies, waits for them, and re-layouts  4.83 us

profile of v2, /device:TPU:9, one launch (start us, length us, event | category | flops | bytes accessed | tf_op | source)
XLA Modules:
  0.0 153.0 jit_solution(6963180749941875069)
XLA Ops:
  0.6 1.4 copy.12
  2.0 147.5 %clip_step.1 = (bf16[32,4,1152]{2,1,0:T(4,128)(2,1)}, bf16[128,1152]{1,0:T(8,128)(2,1)}, f32[18,1152]{1,0:T(8,128)}) custom-call(bf16[128,1152]{1,0:T(8,128)(2,1)} %bitcast.10, f32[6,1152]{1,0:T(8,128)} %bitcast.9, bf16[36,1728]{1,0:T(8,128)(2,1)} %space_project.1, bf16[18,1152]{1,0:T(8,128)(2,1)} %space_merge.1, bf16[36,1728]{1,0:T(8,128)(2,1)} %time_project.1, ...), custom_call_target="tpu_custom_call" | custom-call | flops 3000000000 | bytes 4000000 | tf_op jit(solution)/shard_map/clip_step/pallas_call | solution.py:769
  149.5 0.0 copy-start
  149.5 1.8 %copy.16 = bf16[1,16,2,4,1152]{4,3,2,1,0:T(4,128)(2,1)} copy(bf16[1,16,2,4,1152]{4,3,2,1,0:T(4,128)(2,1)} %bitcast.8) | data formatting | bytes 589824
  151.3 0.0 copy-done
  151.3 0.0 copy-start.1
  151.3 0.7 copy.17
  152.1 0.3 copy-done.1
  152.3 0.6 copy.18
Async XLA Ops:
  149.5 1.8 %copy-start = (bf16[128,1152]{1,0:T(8,128)(2,1)S(1)}, bf16[128,1152]{1,0:T(8,128)(2,1)}, u32[]{:S(2)}) copy-start(bf16[128,1152]{1,0:T(8,128)(2,1)} %get-tuple-element.7) | copy-start | bytes 884740
  151.3 1.0 copy-start.1

commit v3 on v2

--- a/solution.py
+++ b/solution.py
@@ -40,6 +40,12 @@
     def y_to(self, step):
         return self.device(y=self.y_at(step))
 
+    def x_at(self, step):
+        return lax.rem(self.x + step + 4, 4)
+
+    def x_to(self, step):
+        return self.device(x=self.x_at(step))
+
     def z_to(self, step):
         return self.device(z=lax.rem(self.z + step + RING, RING))
 
@@ -90,110 +96,165 @@
         self.started = []
 
 
-def gather_y_first(place, link, held, first, other, count):
-    way = place.way
-    up, down = place.y_to(1), place.y_to(-1)
-    above, below = place.z_to(1), place.z_to(-1)
-    sibling = place.sibling()
-
-    def one(step):
-        return held.at[place.low, place.y_at(step), pl.ds(first, count)]
-
-    def ring(step, start):
-        return held.at[place.low_at(step), :, pl.ds(start, count)]
-
-    def go(ref, device):
-        return link.send(ref, ref, device)
-
-    plus, minus = go(one(0), up), go(one(0), down)
-    yield
-    for step in (1, 2):
-        link.arrived(plus, one(-step), up)
-        plus = go(one(-step), up)
-        link.arrived(minus, one(step), down)
-        minus = go(one(step), down)
-        yield
-    link.arrived(plus, one(-3), up)
-    link.arrived(minus, one(3), down)
-    last = go(one(-3 * way), place.y_to(way))
-    yield
-    link.arrived(last, one(4), up)
-    plus, minus = go(ring(0, first), above), go(ring(0, first), below)
-    shared = [(go(ring(0, first), sibling), 0)]
-    yield
-    link.arrived(plus, ring(-1, first), above)
-    link.arrived(minus, ring(1, first), below)
-    last = go(ring(-way, first), place.z_to(way))
-    shared.append((go(ring(-1, first), sibling), -1))
-    shared.append((go(ring(1, first), sibling), 1))
-    yield
-    link.arrived(last, ring(2, first), above)
-    shared.append((go(ring(2, first), sibling), 2))
-    yield
-    for number, step in shared:
-        link.arrived(number, ring(step, other), sibling)
-    yield
-
-
-def gather_z_first(place, link, held, first, other, count):
-    way = place.way
-    up, down = place.y_to(1), place.y_to(-1)
-    above, below = place.z_to(1), place.z_to(-1)
-    sibling = place.sibling()
-
-    def one(step):
-        return held.at[place.low_at(step), place.y, pl.ds(first, count)]
-
-    def run(step, start):
-        return held.at[:, place.y_at(step), pl.ds(start, count)]
-
-    def go(ref, device):
-        return link.send(ref, ref, device)
-
-    plus, minus = go(one(0), above), go(one(0), below)
-    yield
-    link.arrived(plus, one(-1), above)
-    link.arrived(minus, one(1), below)
-    last = go(one(-way), place.z_to(way))
-    yield
-    link.arrived(last, one(2), above)
-    plus, minus = go(run(0, first), up), go(run(0, first), down)
-    shared = [(go(run(0, first), sibling), 0)]
-    yield
-    for step in (1, 2):
-        link.arrived(plus, run(-step, first), up)
-        plus = go(run(-step, first), up)
-        link.arrived(minus, run(step, first), down)
-        minus = go(run(step, first), down)
-        shared.append((go(run(-step, first), sibling), -step))
-        shared.append((go(run(step, first), sibling), step))
-        yield
-    link.arrived(plus, run(-3, first), up)
-    link.arrived(minus, run(3, first), down)
-    last = go(run(-3 * way, first), place.y_to(way))
-    shared.append((go(run(-3, first), sibling), -3))
-    shared.append((go(run(3, first), sibling), 3))
-    yield
-    link.arrived(last, run(4, first), up)
-    shared.append((go(run(4, first), sibling), 4))
-    yield
-    for number, step in shared:
-        link.arrived(number, run(step, other), sibling)
-    yield
-
-
-def gather(place, link, held, begin, y_count, z_count):
-    half = y_count + z_count
-    mine, other = begin + place.core * half, begin + (1 - place.core) * half
-    plans = [
-        gather_y_first(place, link, held, mine, other, y_count),
-        gather_z_first(place, link, held, mine + y_count, other + y_count, z_count),
-    ]
-    while plans:
-        for plan in list(plans):
-            if next(plan, plans) is plans:
-                plans.remove(plan)
-        yield
+class Gather:
+    def __init__(self, place, link, held, begin, sliced, y_count, z_count):
+        self.place, self.link, self.held = place, link, held
+        self.begin, self.sliced = begin, sliced
+        self.rest = begin + 8 * sliced
+        self.y_count, self.z_count = y_count, z_count
+        self.size = 8 * sliced + 2 * (y_count + z_count)
+
+    def slice_of(self, x, core):
+        return pl.ds(self.begin + (x * 2 + core) * self.sliced, self.sliced)
+
+    def y_part(self, core):
+        return pl.ds(self.rest + core * (self.y_count + self.z_count), self.y_count)
+
+    def z_part(self, core):
+        return pl.ds(
+            self.rest + core * (self.y_count + self.z_count) + self.y_count, self.z_count
+        )
+
+    def hold_own(self, local):
+        place, held = self.place, self.held
+        for count, tiles in (
+            (self.sliced, self.slice_of(place.x, place.core)),
+            (self.y_count, self.y_part(place.core)),
+            (self.z_count, self.z_part(place.core)),
+        ):
+            if count:
+                held[place.low, place.y, tiles] = local[tiles]
+
+    def go(self, ref, device):
+        return self.link.send(ref, ref, device)
+
+    def across_y(self, tiles):
+        place = self.place
+        return [
+            (self.go(self.held.at[place.low, place.y, tiles], place.y_to(step)), step)
+            for step in range(1, RING)
+        ]
+
+    def arrived_y(self, numbers, tiles):
+        place = self.place
+        for number, step in numbers:
+            self.link.arrived(
+                number, self.held.at[place.low, place.y_at(-step), tiles], place.y_to(step)
+            )
+
+    def across_z(self, part):
+        place = self.place
+        return [
+            (self.go(part(0), place.z_to(1)), -1),
+            (self.go(part(0), place.z_to(-1)), 1),
+            (self.go(part(0), place.z_to(2 * place.way)), 2),
+        ]
+
+    def arrived_z(self, numbers, part):
+        for number, step in numbers:
+            self.link.arrived(number, part(step), self.place.z_to(1))
+
+    def share(self, refs):
+        return [self.go(ref, self.place.sibling()) for ref in refs]
+
+    def shared(self, numbers, refs):
+        for number, ref in zip(numbers, refs, strict=True):
+            self.link.arrived(number, ref, self.place.sibling())
+
+    def over_x(self):
+        place, held = self.place, self.held
+        mine = self.slice_of(place.x, place.core)
+
+        def ring(step):
+            return held.at[place.low_at(step), :, mine]
+
+        def whole(step, core):
+            return held.at[:, :, self.slice_of(place.x_at(step), core)]
+
+        numbers = self.across_y(mine)
+        yield
+        self.arrived_y(numbers, mine)
+        numbers = self.across_z(ring)
+        yield
+        self.arrived_z(numbers, ring)
+        block = whole(0, place.core)
+        plus, minus = self.go(block, place.x_to(1)), self.go(block, place.x_to(-1))
+        given = self.share([block])
+        yield
+        self.link.arrived(plus, whole(-1, place.core), place.x_to(1))
+        self.link.arrived(minus, whole(1, place.core), place.x_to(-1))
+        last = self.go(whole(-place.way, place.core), place.x_to(place.way))
+        given += self.share([whole(-1, place.core), whole(1, place.core)])
+        yield
+        self.link.arrived(last, whole(2, place.core), place.x_to(1))
+        given += self.share([whole(2, place.core)])
+        yield
+        self.shared(given, [whole(step, 1 - place.core) for step in (0, -1, 1, 2)])
+        yield
+
+    def y_first(self):
+        place, held = self.place, self.held
+        mine, other = self.y_part(place.core), self.y_part(1 - place.core)
+
+        def ring(step):
+            return held.at[place.low_at(step), :, mine]
+
+        numbers = self.across_y(mine)
+        yield
+        self.arrived_y(numbers, mine)
+        numbers = self.across_z(ring)
+        given = self.share([ring(0)])
+        yield
+        self.arrived_z(numbers, ring)
+        given += self.share([ring(step) for step in (-1, 1, 2)])
+        yield
+        self.shared(given, [held.at[place.low_at(step), :, other] for step in (0, -1, 1, 2)])
+        yield
+
+    def z_first(self):
+        place, held = self.place, self.held
+        mine, other = self.z_part(place.core), self.z_part(1 - place.core)
+
+        def one(step):
+            return held.at[place.low_at(step), place.y, mine]
+
+        def run(step):
+            return held.at[:, place.y_at(step), mine]
+
+        numbers = self.across_z(one)
+        yield
+        self.arrived_z(numbers, one)
+        near = (1, -1, 2, -2)
+        numbers = [self.go(run(0), place.y_to(step)) for step in near]
+        given = self.share([run(0)])
+        yield
+        for number, step in zip(numbers, near, strict=True):
+            self.link.arrived(number, run(-step), place.y_to(step))
+        numbers = [
+            self.go(run(-2), place.y_to(1)),
+            self.go(run(2), place.y_to(-1)),
+            self.go(run(-2 * place.way), place.y_to(2 * place.way)),
+        ]
+        given += self.share([run(-step) for step in near])
+        yield
+        far = (-3, 3, 4)
+        for number, step in zip(numbers, far, strict=True):
+            self.link.arrived(number, run(step), place.y_to(1))
+        given += self.share([run(step) for step in far])
+        yield
+        steps = (0,) + tuple(-step for step in near) + far
+        self.shared(given, [held.at[:, place.y_at(step), other] for step in steps])
+        yield
+
+    def plan(self):
+        plans = [self.over_x()] if self.sliced else []
+        plans += [self.z_first()] if self.z_count else []
+        plans += [self.y_first()] if self.y_count else []
+        while plans:
+            for plan in list(plans):
+                if next(plan, plans) is plans:
+                    plans.remove(plan)
+            yield
 
 
 def lane_tiles(width):
@@ -218,11 +279,6 @@
         ]
     for group in range(groups):
         local[number + group] = staged[group].astype(jnp.bfloat16)
-
-
-def hold_own(place, local, held, begin, count):
-    mine = pl.ds(begin + place.core * (count // 2), count // 2)
-    held[place.low, place.y, mine] = local[mine]
 
 
 def unpack_all(held, begin, rows, width, stage, out):
@@ -262,73 +318,85 @@
 
 PROJECT_TILES, MERGE_TILES = 32, 12
 HELD_TILES = 2 * (PROJECT_TILES + MERGE_TILES)
-GATHER_COPIES = 32
-REDUCE_COPIES = 16
-
-
-def reduce_plan(place, link, packed, near, total, long_out, long_in, short_out, short_in, small, final):
-    way, half = place.way, MERGE_TILES // 2
+GATHER_COPIES = 52
+REDUCE_COPIES = 32
+
+
+Z_TILES = 4
+
+
+def reduce_plan(place, link, packed, near, total, z_in, z_sum, zy_in, y_in, y_sum, yz_in, parts, final):
+    half = MERGE_TILES // 2
     mine, other = place.core * half, (1 - place.core) * half
     sibling = place.sibling()
+    first, second = pl.ds(0, Z_TILES), pl.ds(Z_TILES, half - Z_TILES)
+    f32, b16 = jnp.float32, jnp.bfloat16
+    lows = ((1, 1), (-1, -1), (2, 2 * place.way))
     number = link.send(packed.at[:, :, pl.ds(other, half)], near, sibling)
     yield
     link.arrived(number, near, sibling)
 
     def add(low, carry):
         for y in range(RING):
-            total[low, y] = packed[low, y, pl.ds(mine, half)].astype(jnp.float32) + near[
-                low, y
-            ].astype(jnp.float32)
+            total[low, y] = (
+                packed[low, y, pl.ds(mine, half)].astype(f32) + near[low, y].astype(f32)
+            ).astype(b16)
         return carry
 
     lax.fori_loop(0, LOW, add, 0)
-    there, back = place.y_to(way), place.y_to(-way)
-    for step in range(4):
-        value = total[:, place.y_at((4 - step) * way)]
-        if step:
-            link.arrived(long_number, long_in.at[step - 1], there)
-            value = value + long_in[step - 1].astype(jnp.float32)
-        long_out[step] = value.astype(jnp.bfloat16)
-        long_number = link.send(long_out.at[step], long_in.at[step], there)
-        if step < 3:
-            value = total[:, place.y_at((step - 3) * way)]
-            if step:
-                link.arrived(short_number, short_in.at[step - 1], back)
-                value = value + short_in[step - 1].astype(jnp.float32)
-            short_out[step] = value.astype(jnp.bfloat16)
-            short_number = link.send(short_out.at[step], short_in.at[step], back)
-        yield
-    link.arrived(short_number, short_in.at[2], back)
-    link.arrived(long_number, long_in.at[3], there)
-    small[pl.ds(0, 4)] = (
-        total[:, place.y] + long_in[3].astype(jnp.float32) + short_in[2].astype(jnp.float32)
-    )
-    parity, upper = lax.rem(place.low, 2), lax.div(place.low, 2)
-    device = place.device(z=place.z + 1 - 2 * parity)
-    numbers = [
-        link.send(small.at[1 - parity + 2 * k], small.at[4 + k], device) for k in range(2)
+    z_numbers = [
+        link.send(total.at[place.low_at(step), :, first], z_in.at[slot], place.z_to(hops))
+        for slot, (step, hops) in enumerate(lows)
+    ]
+    y_numbers = [
+        link.send(total.at[:, place.y_at(step), second], y_in.at[step - 1], place.y_to(step))
+        for step in range(1, RING)
     ]
     yield
-    for k in range(2):
-        link.arrived(numbers[k], small.at[4 + k], device)
-        small[6 + k] = small[parity + 2 * k] + small[4 + k]
-    device = place.device(z=place.z + 2 - 4 * upper)
-    number = link.send(small.at[7 - upper], small.at[8], device)
+    value = total[place.low, :, first].astype(f32)
+    for slot, number in enumerate(z_numbers):
+        link.arrived(number, z_in.at[slot], sibling)
+        value = value + z_in[slot].astype(f32)
+    z_sum[...] = value.astype(b16)
+    z_numbers = [
+        link.send(z_sum.at[place.y_at(step)], zy_in.at[step - 1], place.y_to(step))
+        for step in range(1, RING)
+    ]
+    value = total[:, place.y, second].astype(f32)
+    for slot, number in enumerate(y_numbers):
+        link.arrived(number, y_in.at[slot], sibling)
+        value = value + y_in[slot].astype(f32)
+    y_sum[...] = value.astype(b16)
+    y_numbers = [
+        link.send(y_sum.at[place.low_at(step)], yz_in.at[slot], place.z_to(hops))
+        for slot, (step, hops) in enumerate(lows)
+    ]
     yield
-    link.arrived(number, small.at[8], device)
-    small[9] = small[6 + upper] + small[8]
-    at = 9
-    for device in (
-        place.device(z=lax.rem(place.z + LOW, RING)),
-        place.device(x=place.x + 1 - 2 * lax.rem(place.x, 2)),
-        place.device(x=lax.rem(place.x + 2, 4)),
-    ):
-        number = link.send(small.at[at], small.at[at + 1], device)
-        yield
-        link.arrived(number, small.at[at + 1], device)
-        small[at + 2] = small[at] + small[at + 1]
-        at += 2
-    final[pl.ds(mine, half)] = small[at]
+    value = z_sum[place.y].astype(f32)
+    for slot, number in enumerate(z_numbers):
+        link.arrived(number, zy_in.at[slot], sibling)
+        value = value + zy_in[slot].astype(f32)
+    me = place.x * 2 + place.high
+    parts[me, first] = value.astype(b16)
+    value = y_sum[place.low].astype(f32)
+    for slot, number in enumerate(y_numbers):
+        link.arrived(number, yz_in.at[slot], sibling)
+        value = value + yz_in[slot].astype(f32)
+    parts[me, second] = value.astype(b16)
+    numbers = []
+    for step in range(1, 8):
+        there = lax.rem(me + step, 8)
+        device = place.device(
+            x=lax.div(there, 2), z=lax.rem(there, 2) * LOW + place.low
+        )
+        numbers.append(link.send(parts.at[me], parts.at[me], device))
+    yield
+    for step, number in enumerate(numbers, 1):
+        link.arrived(number, parts.at[lax.rem(me - step + 8, 8)], sibling)
+    value = parts[0].astype(f32)
+    for index in range(1, 8):
+        value = value + parts[index].astype(f32)
+    final[pl.ds(mine, half)] = value
     number = link.send(final.at[pl.ds(mine, half)], final.at[pl.ds(mine, half)], sibling)
     yield
     link.arrived(number, final.at[pl.ds(other, half)], sibling)
@@ -484,14 +552,14 @@
     outer = lax.axis_index("dp")
     me = lax.axis_index("seq")
     listed = [(outer, lax.rem(me + away, MEMBERS)) for away in range(1, MEMBERS)]
-    return listed + [
-        place.sibling(),
-        place.z_to(1),
-        place.z_to(-1),
-        place.z_to(LOW),
-        place.device(x=place.x + 1 - 2 * lax.rem(place.x, 2)),
-        place.device(x=lax.rem(place.x + 2, 4)),
-    ]
+    listed += [place.z_to(step) for step in (1, -1, 2, -2)]
+    slot = place.x * 2 + place.high
+    for step in range(1, 8):
+        there = lax.rem(slot + step, 8)
+        listed.append(
+            place.device(x=lax.div(there, 2), z=lax.rem(there, 2) * LOW + place.low)
+        )
+    return listed + [place.sibling()]
 
 
 def advance(plans, rounds=1000):
@@ -533,12 +601,14 @@
         "part": pltpu.VMEM(merge, f32),
         "packed_part": pltpu.VMEM((LOW, RING, MERGE_TILES) + TILE, b16),
         "near": pltpu.VMEM((LOW, RING, half) + TILE, b16),
-        "total": pltpu.VMEM((LOW, RING, half) + TILE, f32),
-        "long_out": pltpu.VMEM((4, LOW, half) + TILE, b16),
-        "long_in": pltpu.VMEM((4, LOW, half) + TILE, b16),
-        "short_out": pltpu.VMEM((3, LOW, half) + TILE, b16),
-        "short_in": pltpu.VMEM((3, LOW, half) + TILE, b16),
-        "small": pltpu.VMEM((16, half) + TILE, f32),
+        "total": pltpu.VMEM((LOW, RING, half) + TILE, b16),
+        "z_in": pltpu.VMEM((3, RING, Z_TILES) + TILE, b16),
+        "z_sum": pltpu.VMEM((RING, Z_TILES) + TILE, b16),
+        "zy_in": pltpu.VMEM((RING - 1, Z_TILES) + TILE, b16),
+        "y_in": pltpu.VMEM((RING - 1, LOW, half - Z_TILES) + TILE, b16),
+        "y_sum": pltpu.VMEM((LOW, half - Z_TILES) + TILE, b16),
+        "yz_in": pltpu.VMEM((3, half - Z_TILES) + TILE, b16),
+        "parts": pltpu.VMEM((8, half) + TILE, b16),
         "final": pltpu.VMEM((MERGE_TILES,) + TILE, f32),
         "reduce_sent": sems((REDUCE_COPIES,)),
         "reduce_come": sems((REDUCE_COPIES,)),
@@ -617,47 +687,50 @@
     starts = (0, PROJECT_TILES, PROJECT_TILES + MERGE_TILES, 2 * PROJECT_TILES + MERGE_TILES)
     for shard, start in zip((space_project, space_merge, time_project, time_merge), starts):
         pack_own(shard, at.staged, at.loose, at.local, start)
-    hold_own(place, at.local, at.held, 0, 32)
-    hold_own(place, at.local, at.held, starts[1], 12)
-    hold_own(place, at.local, at.held, starts[2], 44)
     at.both_tokens[0] = tokens[...]
     links = [Link(at.gather_sent.at[i], at.gather_come.at[i]) for i in range(3)]
-    first = [gather(place, links[0], at.held, 0, 9, 7)]
-    later = [
-        gather(place, links[1], at.held, starts[1], 4, 2),
-        gather(place, links[2], at.held, starts[2], 13, 9),
+    groups = [
+        Gather(place, links[0], at.held, starts[0], 2, 3, 5),
+        Gather(place, links[1], at.held, starts[1], 1, 1, 1),
+        Gather(place, links[2], at.held, starts[2], 2, 6, 8),
     ]
+    for group in groups:
+        group.hold_own(at.local)
+    plans = {name: [group.plan()] for name, group in zip("SMT", groups)}
+
+    def steps(order):
+        for name in order:
+            advance(plans[name], 1)
+
     pl.semaphore_wait(pltpu.get_barrier_semaphore(), expected)
-    advance(first, 1)
+    steps("SMT")
     pair = Link(at.pair_sent, at.pair_come)
     partner = place.y_to(1 - 2 * lax.rem(place.y, 2))
     number = pair.send(at.both_tokens.at[0], at.both_tokens.at[1], partner)
-    advance(first, 1)
-    advance(later, 1)
     normed, inverse_std = normalize(tokens[...].astype(jnp.float32))
     at.space_normed[...] = normed
     at.space_inverse[...] = inverse_std
     at.modulated[:TOKENS] = (normed * (1.0 + row(1)) + row(0)).astype(jnp.bfloat16)
     from_blocks(cotangent, at.grad_result)
-    advance(first, 1)
+    steps("SM")
     pair.arrived(number, at.both_tokens.at[1], partner)
     normed, _ = normalize(at.both_tokens[1].astype(jnp.float32))
     at.modulated[TOKENS:] = (normed * (1.0 + row(1)) + row(0)).astype(jnp.bfloat16)
-    while first:
-        advance(first, 1)
-        advance(later, 1)
+    steps("SMTSMSM")
+    advance(plans["S"])
     unpack_all(at.held, starts[0], 36, 1728, at.stage, at.space_project)
 
     at.packed[:, : 3 * INNER] = dot(at.modulated[...], at.space_project[...])
     split_packed(at.packed, 2 * TOKENS, at.space_queries, at.space_keys, at.space_values)
-    advance(later, 1)
+    steps("T")
     attend(at.space_queries, at.space_keys, at.space_values, at.space_probs, at.attended)
-    advance(later)
+    advance(plans["M"])
     unpack_all(at.held, starts[1], 18, 1152, at.stage, at.space_merge)
     branch = dot(at.attended[...].astype(jnp.bfloat16), at.space_merge[...])
     at.wide[...] = tokens[...].astype(jnp.float32) + row(2) * branch
     to_blocks(at.wide, at.middle_out)
     trade_start(at.middle_out, at.middle_in, at.middle_sent, at.middle_come)
+    advance(plans["T"])
     unpack_all(at.held, starts[2], 36, 1728, at.stage, at.time_project)
     unpack_all(at.held, starts[3], 18, 1152, at.stage, at.time_merge)
     scaled = (row(5) * at.grad_result[...]).astype(jnp.bfloat16)
@@ -688,8 +761,8 @@
     reducing = Link(at.reduce_sent, at.reduce_come)
     reduction = [
         reduce_plan(
-            place, reducing, at.packed_part, at.near, at.total, at.long_out, at.long_in,
-            at.short_out, at.short_in, at.small, at.final,
+            place, reducing, at.packed_part, at.near, at.total, at.z_in, at.z_sum, at.zy_in,
+            at.y_in, at.y_sum, at.yz_in, at.parts, at.final,
         )
     ]
     advance(reduction, 1)

time: 153 us -> 121 us (0.79)
  the two profiles are of different devices: /device:TPU:9 before, /device:TPU:1 now
where the time goes in v3:
time: 121 us; the launch traced here: 120 us
  Pallas kernels  115 us (95%)
  local copies, waits for them, and re-layouts  4.83 us (4%)
    pallas_call x1, Pallas kernels, body(): pl.pallas_call(clip_kernel, out_shape=[jax.ShapeDtypeStruct(blocks, jnp.b...  115 us
    unnamed x8, local copies, waits for them, and re-layouts  4.83 us

profile of v3, /device:TPU:1, one launch (start us, length us, event | category | flops | bytes accessed | tf_op | source)
XLA Modules:
  0.0 120.3 jit_solution(12007227271434801972)
XLA Ops:
  0.6 1.4 %copy.12 = f32[1,6,1152]{2,1,0:T(8,128)} copy(f32[1,6,1152]{2,0,1:T(1,128)} %param.8) | data formatting | bytes 55296
  2.0 114.8 %clip_step.1 = (bf16[32,4,1152]{2,1,0:T(4,128)(2,1)}, bf16[128,1152]{1,0:T(8,128)(2,1)}, f32[18,1152]{1,0:T(8,128)}) custom-call(bf16[128,1152]{1,0:T(8,128)(2,1)} %bitcast.10, f32[6,1152]{1,0:T(8,128)} %bitcast.9, bf16[36,1728]{1,0:T(8,128)(2,1)} %space_project.1, bf16[18,1152]{1,0:T(8,128)(2,1)} %space_merge.1, bf16[36,1728]{1,0:T(8,128)(2,1)} %time_project.1, ...), custom_call_target="tpu_custom_call" | custom-call | flops 3000000000 | bytes 4000000 | tf_op jit(solution)/shard_map/clip_step/pallas_call | solution.py:842
  116.8 0.0 copy-start
  116.8 1.8 %copy.16 = bf16[1,16,2,4,1152]{4,3,2,1,0:T(4,128)(2,1)} copy(bf16[1,16,2,4,1152]{4,3,2,1,0:T(4,128)(2,1)} %bitcast.8) | data formatting | bytes 589824
  118.6 0.0 copy-done
  118.6 0.0 copy-start.1
  118.6 0.7 copy.17
  119.4 0.3 copy-done.1
  119.6 0.6 copy.18
Async XLA Ops:
  116.8 1.8 %copy-start = (bf16[128,1152]{1,0:T(8,128)(2,1)S(1)}, bf16[128,1152]{1,0:T(8,128)(2,1)}, u32[]{:S(2)}) copy-start(bf16[128,1152]{1,0:T(8,128)(2,1)} %get-tuple-element.7) | copy-start | bytes 884740
  118.6 1.0 copy-start.1

commit v4 on v3

--- a/solution.py
+++ b/solution.py
@@ -479,7 +479,7 @@
         raised = jnp.exp(scores - jnp.max(scores, -1, keepdims=True))
         probs = raised * (1.0 / jnp.sum(raised, -1, keepdims=True))
         probs_ref[head] = probs
-        attended[:, window] += dot(probs.astype(jnp.bfloat16), values[:, window] * own)
+        attended[:, window] += dot(probs[:TOKENS].astype(jnp.bfloat16), values[:, window] * own)
 
 
 def score_grads(grad_attended, own, window, values, probs):
@@ -572,7 +572,7 @@
 
 
 def split_packed(packed, rows, queries, keys, values):
-    queries[...] = packed[:TOKENS, :INNER].astype(jnp.bfloat16)
+    queries[...] = packed[:rows, :INNER].astype(jnp.bfloat16)
     keys[...] = packed[:rows, INNER : 2 * INNER].astype(jnp.bfloat16)
     values[...] = packed[:rows, 2 * INNER : 3 * INNER].astype(jnp.bfloat16)
 
@@ -617,10 +617,10 @@
         "packed": pltpu.VMEM((2 * TOKENS, 1792), f32),
         "space_normed": pltpu.VMEM(wide, f32),
         "space_inverse": pltpu.VMEM((TOKENS, 1), f32),
-        "space_queries": pltpu.VMEM(narrow, b16),
+        "space_queries": pltpu.VMEM((2 * TOKENS, INNER), b16),
         "space_keys": pltpu.VMEM((2 * TOKENS, INNER), b16),
         "space_values": pltpu.VMEM((2 * TOKENS, INNER), b16),
-        "space_probs": pltpu.VMEM((HEADS, TOKENS, 2 * TOKENS), f32),
+        "space_probs": pltpu.VMEM((HEADS, 2 * TOKENS, 2 * TOKENS), f32),
         "attended": pltpu.VMEM(narrow, f32),
         "time_normed": pltpu.VMEM(wide, f32),
         "time_queries": pltpu.VMEM(narrow, b16),
@@ -631,13 +631,12 @@
         "across": pltpu.VMEM(wide, f32),
         "grad_result": pltpu.VMEM(wide, f32),
         "grad_attended": pltpu.VMEM(narrow, b16),
-        "grad_scores": pltpu.VMEM((HEADS, TOKENS, 2 * TOKENS), b16),
         "grad_queries": pltpu.VMEM(narrow, f32),
-        "grad_keys": pltpu.VMEM((2 * TOKENS, INNER), f32),
-        "grad_values": pltpu.VMEM((2 * TOKENS, INNER), f32),
+        "grad_keys": pltpu.VMEM(narrow, f32),
+        "grad_values": pltpu.VMEM(narrow, f32),
         "grad_packed": pltpu.VMEM((TOKENS, 1792), f32),
-        "far_out": pltpu.VMEM((2,) + narrow, b16),
-        "far_in": pltpu.VMEM((2,) + narrow, b16),
+        "far_attended": pltpu.VMEM(narrow, b16),
+        "near_attended": pltpu.VMEM(narrow, b16),
         "middle_out": pltpu.VMEM(blocks, b16),
         "middle_in": pltpu.VMEM(blocks, b16),
         "grad_out": pltpu.VMEM(blocks, b16),
@@ -682,7 +681,7 @@
     expected = greet(partners(place))
 
     def row(index):
-        return modulation[index : index + 1, :]
+        return modulation[0, index : index + 1, :]
 
     starts = (0, PROJECT_TILES, PROJECT_TILES + MERGE_TILES, 2 * PROJECT_TILES + MERGE_TILES)
     for shard, start in zip((space_project, space_merge, time_project, time_merge), starts):
@@ -776,13 +775,13 @@
     for head, window, own in head_windows():
         probs = at.time_probs[head]
         grads = score_grads(at.grad_attended, own, window, at.time_values, probs)
-        at.grad_values[:TOKENS, window] += dot_rows(
+        at.grad_values[:, window] += dot_rows(
             probs.astype(jnp.bfloat16), at.grad_attended[:, window] * own
         )
-        at.grad_keys[:TOKENS, window] += dot_rows(grads, at.time_queries[:, window] * own)
+        at.grad_keys[:, window] += dot_rows(grads, at.time_queries[:, window] * own)
         at.grad_queries[:, window] += dot(grads, at.time_keys[:, window] * own)
     grad_packed = join_packed(
-        at.grad_packed, at.grad_queries[...], at.grad_keys[:TOKENS], at.grad_values[:TOKENS]
+        at.grad_packed, at.grad_queries[...], at.grad_keys[...], at.grad_values[...]
     )
     grad_modulated = dot_lanes(grad_packed, at.time_project[...])
     at.wide[...] = at.grad_result[...] + modulate_back(
@@ -795,32 +794,31 @@
     from_blocks(at.grad_in, at.wide)
 
     scaled = (row(2) * at.wide[...]).astype(jnp.bfloat16)
-    at.grad_attended[...] = dot_lanes(scaled, at.space_merge[...]).astype(jnp.bfloat16)
+    at.near_attended[...] = dot_lanes(scaled, at.space_merge[...]).astype(jnp.bfloat16)
+    number = pair.send(at.near_attended, at.far_attended, partner)
     at.grad_keys[...] = jnp.zeros_like(at.grad_keys)
     at.grad_values[...] = jnp.zeros_like(at.grad_values)
     at.grad_queries[...] = jnp.zeros_like(at.grad_queries)
-    far = pl.ds(TOKENS, TOKENS)
-    for head, window, own in head_windows():
-        probs = at.space_probs[head]
-        grads = score_grads(at.grad_attended, own, window, at.space_values, probs)
-        at.grad_scores[head] = grads
-        at.grad_values[:, window] += dot_rows(
-            probs.astype(jnp.bfloat16), at.grad_attended[:, window] * own
-        )
-        at.grad_keys[:, window] += dot_rows(grads, at.space_queries[:, window] * own)
-    at.far_out[0] = at.grad_keys[far, :].astype(jnp.bfloat16)
-    at.far_out[1] = at.grad_values[far, :].astype(jnp.bfloat16)
-    number = pair.send(at.far_out, at.far_in, partner)
-    advance(reduction, 1)
-    for head, window, own in head_windows():
-        at.grad_queries[:, window] += dot(at.grad_scores[head], at.space_keys[:, window] * own)
-    advance(reduction, 1)
-    pair.arrived(number, at.far_in, partner)
+    for rows, grad_attended in (
+        (slice(0, TOKENS), at.near_attended),
+        (slice(TOKENS, 2 * TOKENS), at.far_attended),
+    ):
+        if rows.start:
+            advance(reduction, 1)
+            pair.arrived(number, at.far_attended, partner)
+        for head, window, own in head_windows():
+            probs = at.space_probs[head, rows, :]
+            grads = score_grads(grad_attended, own, window, at.space_values, probs)
+            at.grad_values[:, window] += dot_rows(
+                probs[:, :TOKENS].astype(jnp.bfloat16), grad_attended[:, window] * own
+            )
+            at.grad_keys[:, window] += dot_rows(
+                grads[:, :TOKENS], at.space_queries[rows, window] * own
+            )
+            if not rows.start:
+                at.grad_queries[:, window] += dot(grads, at.space_keys[:, window] * own)
     grad_packed = join_packed(
-        at.grad_packed,
-        at.grad_queries[...],
-        at.grad_keys[:TOKENS] + at.far_in[0].astype(jnp.float32),
-        at.grad_values[:TOKENS] + at.far_in[1].astype(jnp.float32),
+        at.grad_packed, at.grad_queries[...], at.grad_keys[...], at.grad_values[...]
     )
     advance(reduction, 1)
     grad_modulated = dot_lanes(grad_packed, at.space_project[...])
@@ -858,7 +856,7 @@
         name="clip_step",
     )(
         tokens.reshape(TOKENS, MODEL),
-        modulation.reshape(6, MODEL),
+        modulation,
         spatial_project,
         spatial_merge,
         temporal_project,

time: 121 us -> 119 us (0.983)
  Pallas kernels: 115 us -> 113 us
    pallas_call x1, Pallas kernels: 115 us -> 113 us  [body(): pl.pallas_call(clip_kernel, out_shape=[jax.ShapeDtypeStruct(blocks, jnp.b...]
where the time goes in v4:
time: 119 us
  Pallas kernels  113 us (95%)
  local copies, waits for them, and re-layouts  4.83 us (4%)
    pallas_call x1, Pallas kernels, body(): pl.pallas_call(clip_kernel, out_shape=[jax.ShapeDtypeStruct(blocks, jnp.b...  113 us
    unnamed x8, local copies, waits for them, and re-layouts  4.83 us

profile of v4, /device:TPU:1, one launch (start us, length us, event | category | flops | bytes accessed | tf_op | source)
XLA Modules:
  0.0 118.9 jit_solution(15193376534144662462)
XLA Ops:
  0.6 1.4 %copy.10.modulation = f32[1,6,1152]{2,1,0:T(8,128)} copy(f32[1,6,1152]{2,0,1:T(1,128)} %param.8) | data formatting | bytes 55296 | tf_op args[1]
  2.0 113.4 %clip_step.1 = (bf16[32,4,1152]{2,1,0:T(4,128)(2,1)}, bf16[128,1152]{1,0:T(8,128)(2,1)}, f32[18,1152]{1,0:T(8,128)}) custom-call(bf16[128,1152]{1,0:T(8,128)(2,1)} %bitcast.6, f32[1,6,1152]{2,1,0:T(8,128)} %copy.10.modulation, bf16[36,1728]{1,0:T(8,128)(2,1)} %space_project.1, bf16[18,1152]{1,0:T(8,128)(2,1)} %space_merge.1, bf16[36,1728]{1,0:T(8,128)(2,1)} %time_project.1, ...), custom_call_target="tpu_custom_call" | custom-call | flops 3000000000 | bytes 4000000 | tf_op jit(solution)/shard_map/clip_step/pallas_call | solution.py:840
  115.4 0.0 copy-start
  115.4 1.8 %copy.14 = bf16[1,16,2,4,1152]{4,3,2,1,0:T(4,128)(2,1)} copy(bf16[1,16,2,4,1152]{4,3,2,1,0:T(4,128)(2,1)} %bitcast.5) | data formatting | bytes 589824
  117.2 0.0 copy-done
  117.2 0.0 copy-start.1
  117.2 0.7 copy.15
  117.9 0.3 copy-done.1
  118.2 0.6 copy.16
Async XLA Ops:
  115.4 1.8 %copy-start = (bf16[128,1152]{1,0:T(8,128)(2,1)S(1)}, bf16[128,1152]{1,0:T(8,128)(2,1)}, u32[]{:S(2)}) copy-start(bf16[128,1152]{1,0:T(8,128)(2,1)} %get-tuple-element.7) | copy-start | bytes 884740
  117.2 1.0 copy-start.1
